TPU v7x, 512 devices: a whole 4x8x8 slice. The times are simulated.
512 devices in a mesh: dp: 16 (over x, y_hi, core), tensor: 32 (over z, y_lo).
Axes of the slice: x: 4, y: 8 (y_hi: 2, y_lo: 4; y = y_hi * 4 + y_lo), z: 8, core: 2. Of those that a mesh axis runs over, the one named last changes fastest.
Arguments:
- token_ids: int32 [4, 640], P(None, 'dp'), may hold values from 0 to 81919
- lengths: int32 [640], P('dp'), may hold values from 2 to 64, as said below
- embed_table: bfloat16 [16, 32, 16, 81920], P(None, 'tensor', 'dp')
- norm_gain: bfloat16 [8192], P('tensor'), may hold values from 0.5 to 1.5
- w_query: bfloat16 [8192, 8192], P('dp', 'tensor'), may hold values from -0.0625 to 0.0625
- key_value_weight: bfloat16 [8192, 2048], P('dp', 'tensor'), may hold values from -0.0625 to 0.0625
- w_out: bfloat16 [8192, 8192], P('tensor', 'dp'), may hold values from -0.125 to 0.125
- key_value_cache: bfloat16 [640, 32, 16, 256], P('dp', 'tensor'), as said below
Outputs:
- hidden: bfloat16 [4, 640, 8192], P(None, 'dp', 'tensor')
Inputs may be any that keep to these rules, and one draw needn't show every extreme that they name: `lengths`: some row has exactly 64 cached positions. `key_value_cache`: keys are stored already rotated for their positions.
All inputs are finite; a program needn't handle non-finite values.
Results may differ from a plain program's by a relative error of at most 0.024.
Values may be sent and summed in bfloat16 or wider, within the bound.
A program may use at most 128 MiB of HBM per device.

v0:
```python
import math

import jax
import jax.numpy as jnp
from jax import lax
from jax.sharding import PartitionSpec as P

KEY_HEADS = 8


EPS = 1e-06
THETA = 1000000.0


def swapped(shard, axis, stride):
    return lax.ppermute(shard, axis, [(i, i ^ 1 << stride) for i in range(lax.axis_size(axis))])


def rotate(vectors, turn):
    half_width = vectors.shape[-1] // 2
    front_half = vectors[..., :half_width]
    back_half = vectors[..., half_width:]
    cosine = jnp.cos(turn)
    sine_part = jnp.sin(turn)
    return jnp.concatenate(
        [front_half * cosine - back_half * sine_part, back_half * cosine + front_half * sine_part],
        axis=-1,
    )


def angles(positions, half_width):
    frequency = THETA ** (-(jnp.arange(half_width, dtype=jnp.float32) / half_width))
    return positions.astype(jnp.float32)[..., None] * frequency


def double_up(values, join_dim, share_count, quad_place, swapper):
    level = 0
    while 1 << level < share_count:
        partner = swapper(values, level)
        is_upper = quad_place >> level & 1 == 1
        values = jnp.where(
            is_upper,
            jnp.concatenate([partner, values], join_dim),
            jnp.concatenate([values, partner], join_dim),
        )
        level = level + 1
    return values


def body(
    token_ids, lengths, embed_table, norm_gain, w_query, key_value_weight, w_out, key_value_cache
):
    step_count, row_count = token_ids.shape
    tensor_count = lax.axis_size("tensor")
    tensor_place = lax.axis_index("tensor")
    share_count = tensor_count // KEY_HEADS
    quad_place = tensor_place % share_count
    head_dim = key_value_cache.shape[3] // 2
    heads_here = w_query.shape[1] // head_dim

    def swap_cache(values, level):
        return swapped(values, "tensor", level)

    cache_full = double_up(key_value_cache[:, 0], 1, share_count, quad_place, swap_cache)
    all_ids = lax.all_gather(token_ids, "dp", axis=1, tiled=True)
    looked = jnp.take(embed_table[:, 0, 0, :], all_ids.reshape(-1), axis=1)
    feat_block = looked.shape[0]
    looked = looked.reshape(feat_block, step_count, -1, row_count)
    arrived = lax.all_to_all(looked, "dp", split_axis=2, concat_axis=2, tiled=True)
    own_part = jnp.transpose(arrived, (1, 3, 2, 0)).reshape(step_count, row_count, -1)
    own_float = own_part.astype(jnp.float32)
    whole, gain_all = (
        lax.all_gather(own_part, "tensor", axis=2, tiled=True),
        lax.all_gather(norm_gain, "tensor", axis=0, tiled=True),
    )
    whole_float = whole.astype(jnp.float32)
    factor = lax.rsqrt(jnp.mean(whole_float * whole_float, axis=-1, keepdims=True) + EPS)
    normed = (whole_float * factor * gain_all.astype(jnp.float32)).astype(jnp.bfloat16)
    flat_rows = normed.reshape(step_count * row_count, -1)
    query_raw = jnp.dot(
        flat_rows,
        lax.all_gather(w_query, "dp", axis=0, tiled=True),
        preferred_element_type=jnp.float32,
    )
    keyval_raw = jnp.dot(
        flat_rows,
        lax.all_gather(key_value_weight, "dp", axis=0, tiled=True),
        preferred_element_type=jnp.float32,
    )
    positions = lengths[None, :] + jnp.arange(step_count, dtype=jnp.int32)[:, None]
    turn = angles(positions, head_dim // 2)
    query_rows = rotate(
        query_raw.reshape(step_count, row_count, heads_here, head_dim), turn[:, :, None, :]
    ).astype(jnp.bfloat16)
    keyval_cols = keyval_raw.astype(jnp.bfloat16)

    def swap_keys(values, level):
        return swapped(values, "tensor", level)

    keyval_head = double_up(keyval_cols, 1, share_count, quad_place, swap_keys)
    keyval_head = keyval_head.reshape(step_count, row_count, 2 * head_dim)
    key_new = rotate(keyval_head[..., :head_dim].astype(jnp.float32), turn).astype(jnp.bfloat16)
    value_new = keyval_head[..., head_dim:]
    cache_len = cache_full.shape[1]
    cache_keys = cache_full[..., :head_dim]
    cache_vals = cache_full[..., head_dim:]
    inv_root = 1.0 / math.sqrt(head_dim)
    scores_old = (
        jnp.einsum("srgd,rcd->srgc", query_rows, cache_keys, preferred_element_type=jnp.float32)
        * inv_root
    )
    scores_new = (
        jnp.einsum("srgd,trd->srgt", query_rows, key_new, preferred_element_type=jnp.float32)
        * inv_root
    )
    valid_old = (
        jnp.arange(cache_len, dtype=jnp.int32)[None, None, None, :] < lengths[None, :, None, None]
    )
    valid_new = (
        jnp.arange(step_count, dtype=jnp.int32)[None, None, None, :]
        <= jnp.arange(step_count, dtype=jnp.int32)[:, None, None, None]
    )
    scores_old = jnp.where(valid_old, scores_old, -1e30)
    scores_new = jnp.where(valid_new, scores_new, -1e30)
    top_score = jnp.maximum(
        jnp.max(scores_old, axis=-1, keepdims=True), jnp.max(scores_new, axis=-1, keepdims=True)
    )
    exp_old = jnp.exp(scores_old - top_score)
    exp_new = jnp.exp(scores_new - top_score)
    totals = jnp.sum(exp_old, axis=-1, keepdims=True) + jnp.sum(exp_new, axis=-1, keepdims=True)
    probs_old = (exp_old / totals).astype(jnp.bfloat16)
    probs_new = (exp_new / totals).astype(jnp.bfloat16)
    attended = jnp.einsum(
        "srgc,rcd->srgd", probs_old, cache_vals, preferred_element_type=jnp.float32
    )
    attended = attended + jnp.einsum(
        "srgt,trd->srgd", probs_new, value_new, preferred_element_type=jnp.float32
    )
    attended = attended.astype(jnp.bfloat16).reshape(step_count * row_count, heads_here * head_dim)
    partial_out = jnp.dot(
        attended,
        lax.all_gather(w_out, "dp", axis=1, tiled=True),
        preferred_element_type=jnp.float32,
    )
    summed = lax.psum_scatter(
        partial_out.reshape(step_count, row_count, -1).astype(jnp.bfloat16),
        "tensor",
        scatter_dimension=2,
        tiled=True,
    ).astype(jnp.float32)
    return (own_float + summed).astype(jnp.bfloat16)


def solution(mesh):
    in_specs = (
        P(None, "dp"),
        P("dp"),
        P(None, "tensor", "dp", None),
        P("tensor"),
        P("dp", "tensor"),
        P("dp", "tensor"),
        P("tensor", "dp"),
        P("dp", "tensor", None, None),
    )
    out_specs = P(None, "dp", "tensor")
    return jax.shard_map(body, mesh=mesh, in_specs=in_specs, out_specs=out_specs, check_vma=False)
```

profile of v0, /device:TPU:2, one launch (start us, length us, event | category | flops | bytes accessed | tf_op | source)
XLA Modules:
  0.0 647.4 jit_solution(9485522943502711309)
XLA Ops:
  6.5 29.9 %all-gather = s32[16,40,4]{1,2,0:T(4,128)S(1)} all-gather(s32[1,40,4]{1,2,0:T(4,128)} %bitcast.87), channel_id=1, replica_groups=mesh['dp'=16,'tensor'=32] {'dp'}, dimensions={0}, use_global_device_ids=true | all-gather | bytes 10880 | tf_op jit(solution)/shard_map/all_gather | solution.py:65
  36.6 15.0 %copy.132 = bf16[16,1,1,81920]{0,3,2,1:T(8,128)(2,1)} copy(bf16[16,1,1,81920]{3,0,2,1:T(8,128)(2,1)} %param.10) | data formatting | bytes 5242880 | tf_op args[2]
  51.6 13.9 %gather_fusion = bf16[2560,16]{1,0:T(8,128)(2,1)S(1)} fusion(bf16[16,81920]{0,1:T(8,128)(2,1)} %bitcast.72, s32[3072]{0:T(1024)S(1)} %pad_clamp_fusion), kind=kCustom, calls=%fused_computation | custom fusion | bytes 174080 | tf_op jit(solution)/shard_map/jit(_take)/gather | solution.py:66
  66.0 0.4 reshape.181
  66.4 15.7 %all_to_all.5 = bf16[16,2,1280]{2,1,0:T(2,128)(2,1)S(1)} all-to-all(bf16[16,2,1280]{2,1,0:T(2,128)(2,1)S(1)} %reshape.181), channel_id=1, replica_groups=mesh['dp'=16,'tensor'=32] {'dp'}, dimensions={0} | all-to-all | bytes 163840 | tf_op jit(solution)/shard_map/all_to_all | solution.py:69
  82.2 0.4 reshape.182
  82.6 0.8 copy.135
  83.4 0.7 all-gather.11.cloned.1.call-update
  84.2 0.7 all-gather.9.cloned.1.call-update
  84.9 0.5 all-gather.13.cloned.1.call-update
  85.5 1.9 collective-permute-start
  87.5 84.8 %all-gather.1 = bf16[32,1,256]{2,1,0:T(2,128)(2,1)S(1)} all-gather(bf16[1,1,256]{2,1,0:T(2,128)(2,1)S(1)} %reshape.170), channel_id=1, replica_groups=mesh['dp'=16,'tensor'=32] {'tensor'}, dimensions={0}, use_global_device_ids=true | all-gather | bytes 16896 | tf_op jit(solution)/shard_map/all_gather | solution.py:74
  172.7 1.9 collective-permute-start.1
  174.6 66.3 %all-gather.7.cloned.1.call-done = bf16[4,40,8192]{2,1,0:T(8,128)(2,1)} async-done(((bf16[4,40,256]{2,1,0:T(8,128)(2,1)}), bf16[4,40,8192]{2,1,0:T(8,128)(2,1)}) %all-gather.7.cloned.1.call-update) | async-done | bytes 2621456 | tf_op jit(solution)/shard_map/all_gather | solution.py:73
  240.9 2.5 fusion
  243.5 0.7 fusion.2
  244.2 58.0 %all-gather.11.cloned.1.call-done = bf16[8192,64]{0,1:T(8,128)(2,1)} async-done(((bf16[512,64]{0,1:T(8,128)(2,1)}), bf16[8192,64]{0,1:T(8,128)(2,1)}) %all-gather.11.cloned.1.call-update) | async-done | bytes 1048592 | tf_op jit(solution)/shard_map/all_gather | solution.py:87
  302.2 2.2 convolution_convert_fusion.1
  304.4 5.2 collective-permute-start.2
  309.6 3.0 maximum_select_fusion
  312.7 2.9 collective-permute-start.3
  315.8 4.8 collective-permute-done.3
  320.8 0.4 subtract_convert_fusion.1
  321.3 65.3 %all-gather.9.cloned.1.call-done = bf16[8192,256]{1,0:T(8,128)(2,1)} async-done(((bf16[512,256]{1,0:T(8,128)(2,1)}), bf16[8192,256]{1,0:T(8,128)(2,1)}) %all-gather.9.cloned.1.call-update) | async-done | bytes 4194320 | tf_op jit(solution)/shard_map/all_gather | solution.py:82
  386.6 6.4 copy.137
  393.0 3.7 fusion.4
  396.9 0.8 fusion.13
  398.1 1.6 fusion.22
  401.4 66.8 %all-gather.13.cloned.1.call-done = bf16[256,8192]{1,0:T(8,128)(2,1)} async-done(((bf16[256,512]{1,0:T(8,128)(2,1)}), bf16[256,8192]{1,0:T(8,128)(2,1)}) %all-gather.13.cloned.1.call-update) | async-done | bytes 4194320 | tf_op jit(solution)/shard_map/all_gather | solution.py:142
  468.3 4.6 convolution_convert_fusion
  472.9 166.5 %reduce-scatter.2.cloned.1.call-done = bf16[4,40,256]{2,1,0:T(8,128)(2,1)} async-done(((bf16[4,40,8192]{2,1,0:T(8,128)(2,1)}), bf16[4,40,256]{2,1,0:T(8,128)(2,1)}) %reduce-scatter.2.cloned.1.call-update) | async-done | bytes 81936 | tf_op jit(solution)/shard_map/reduce_scatter | solution.py:145
  639.4 1.5 add_convert_fusion
  (68 shorter events, 4.1 us)
Async XLA Ops:
  6.5 234.4 %all-gather.7.cloned.1.call-start = ((), (), s32[]{:S(2)}) async-start(), calls=%async_computation.2 | async-start | bytes 2703360 | tf_op jit(solution)/shard_map/all_gather | solution.py:73
  51.6 33.9 %copy-start.3 = (bf16[40,1,16,256]{3,2,1,0:T(8,128)(2,1)S(1)}, bf16[40,1,16,256]{3,2,1,0:T(8,128)(2,1)}, u32[]{:S(2)}) copy-start(bf16[40,1,16,256]{3,2,1,0:T(8,128)(2,1)} %param.15) | copy-start | bytes 983044
  51.6 35.8 %copy-start.5 = (bf16[256]{0:T(256)(128)(2,1)S(1)}, bf16[256]{0:T(256)(128)(2,1)}, u32[]{:S(2)}) copy-start(bf16[256]{0:T(256)(128)(2,1)} %param.11) | copy-start | bytes 1540
  51.6 120.7 %copy-start.4 = (s32[40]{0:T(128)S(1)}, s32[40]{0:T(128)}, u32[]{:S(2)}) copy-start(s32[40]{0:T(128)} %param.9) | copy-start | bytes 484
  83.4 218.8 %all-gather.11.cloned.1.call-start = ((), (), s32[]{:S(2)}) async-start(), calls=%async_computation.4 | async-start | bytes 1114112 | tf_op jit(solution)/shard_map/all_gather | solution.py:87
  84.2 302.4 %all-gather.9.cloned.1.call-start = ((), (), s32[]{:S(2)}) async-start(), calls=%async_computation.3 | async-start | bytes 4456448 | tf_op jit(solution)/shard_map/all_gather | solution.py:82
  84.9 383.4 %all-gather.13.cloned.1.call-start = ((), (), s32[]{:S(2)}) async-start(), calls=%async_computation.5 | async-start | bytes 4456448 | tf_op jit(solution)/shard_map/all_gather | solution.py:142
  85.5 553.9 %reduce-scatter.2.cloned.1.call-start = ((), (), s32[]{:S(2)}) async-start(), calls=%async_computation.6 | async-start | bytes 2703360 | tf_op jit(solution)/shard_map/reduce_scatter | solution.py:145
  85.5 86.9 %collective-permute-start = (bf16[40,16,256]{2,1,0:T(8,128)(2,1)S(1)}, bf16[40,16,256]{2,1,0:T(8,128)(2,1)S(1)}, u32[]{:S(2)}, u32[]{:S(2)}) collective-permute-start(bf16[40,16,256]{2,1,0:T(8,128)(2,1)S(1)} %bitcast.78), channel_id=1, source_target_pairs={{0,1},{1,0},{2,3},{3,2},{4,5},{5,4},{6,7},{7,6},{8,9},{9,8},{10,11... | collective-permute-start | bytes 983048 | tf_op jit(solution)/shard_map/ppermute | solution.py:16
  172.7 136.9 %collective-permute-start.1 = (bf16[40,32,256]{2,1,0:T(8,128)(2,1)S(1)}, bf16[40,32,256]{2,1,0:T(8,128)(2,1)}, u32[]{:S(2)}, u32[]{:S(2)}) collective-permute-start(bf16[40,32,256]{2,1,0:T(8,128)(2,1)S(1)} %maximum_select_fusion.1), channel_id=1, source_target_pairs={{0,2},{1,3},{2,0},{3,1},{4,6},{5,7},{6,4},{7,5},{8,10},{9,11},{10,... | collective-permute-start | bytes 1966088 | tf_op jit(solution)/shard_map/ppermute | solution.py:16
  240.9 2.5 copy-start
  304.4 8.3 %collective-permute-start.2 = (bf16[160,64]{0,1:T(8,128)(2,1)S(1)}, bf16[160,64]{0,1:T(8,128)(2,1)S(1)}, u32[]{:S(2)}, u32[]{:S(2)}) collective-permute-start(bf16[160,64]{0,1:T(8,128)(2,1)S(1)} %convolution_convert_fusion.1), channel_id=1, source_target_pairs={{0,1},{1,0},{2,3},{3,2},{4,5},{5,4},{6,7},{7,6},{8,9},{9,8},{10,11... | collective-permute-start | bytes 61448 | tf_op jit(solution)/shard_map/ppermute | solution.py:16
  312.7 7.9 %collective-permute-start.3 = (bf16[160,128]{0,1:T(8,128)(2,1)S(1)}, bf16[160,128]{0,1:T(8,128)(2,1)S(1)}, u32[]{:S(2)}, u32[]{:S(2)}) collective-permute-start(bf16[160,128]{0,1:T(8,128)(2,1)S(1)} %maximum_select_fusion.3), channel_id=1, source_target_pairs={{0,2},{1,3},{2,0},{3,1},{4,6},{5,7},{6,4},{7,5},{8,10},{9,11},{10,... | collective-permute-start | bytes 122888 | tf_op jit(solution)/shard_map/ppermute | solution.py:16
  396.7 4.3 copy-start.1
  472.9 166.5 %copy-start.2 = (bf16[4,40,256]{2,1,0:T(8,128)(2,1)S(1)}, bf16[4,40,256]{2,1,0:T(8,128)(2,1)}, u32[]{:S(2)}) copy-start(bf16[4,40,256]{2,1,0:T(8,128)(2,1)} %copy.135) | copy-start | bytes 245764
Sparse Core Ops, SparseCore 0:
  83.5 157.3 all-gather.6
  244.0 58.1 all-gather.10
  305.5 81.0 all-gather.8
  389.5 78.7 all-gather.12
  473.0 166.2 reduce-scatter.1
where the time goes:
time: 648 us; the launch traced here: 647 us
  waiting for transfers between devices  430 us (66%)
  blocking collectives  130 us (20%)
  local copies, waits for them, and re-layouts  38.6 us (6%)
  matrix products  13.5 us (2%)
  between operations  13.5 us (2%)
  starting transfers between devices  12 us (2%)
  other arithmetic  9.79 us (2%)
    reduce_scatter x1, waiting for transfers between devices, body(): lax.psum_scatter(partial_out.reshape(step_count, row_count, -1).astype(jn...  166 us
    all_gather x1, blocking collectives, body(): lax.all_gather(norm_gain, 'tensor', axis=0, tiled=True)  84.8 us
    all_gather x1, waiting for transfers between devices, body(): lax.all_gather(w_out, 'dp', axis=1, tiled=True)  66.8 us
    all_gather x1, waiting for transfers between devices, body(): lax.all_gather(own_part, 'tensor', axis=2, tiled=True)  66.3 us
    all_gather x1, waiting for transfers between devices, body(): lax.all_gather(w_query, 'dp', axis=0, tiled=True)  65.3 us
    all_gather x1, waiting for transfers between devices, body(): lax.all_gather(key_value_weight, 'dp', axis=0, tiled=True)  58 us
    all_gather x1, blocking collectives, body(): all_ids = lax.all_gather(token_ids, 'dp', axis=1, tiled=True)  29.9 us
    unnamed x18, local copies, waits for them, and re-layouts  15.9 us
  transfers between devices with their start and end apart: 9, of which 6 were waited for; matrix products, arithmetic and copies ran while one was open for 4% of the time, Pallas kernels for 0%

commit v1 on v0

v1 whole, which is shorter than its diff:
```python
import functools
import math

import jax
import jax.numpy as jnp
from jax import lax
from jax.experimental import pallas as pl
from jax.experimental.pallas import tpu as pltpu
from jax.sharding import PartitionSpec as P

EPS = 1e-06
THETA = 1000000.0
BF = jnp.bfloat16
F32 = jnp.float32

NX = 4
NZ = 8
NB = 4
QROWS = 40
QPAD = 48
NROWS = 160
XROWS = 176
HEAD = 128
FULL = 8192

MESH = pl.DeviceIdType.MESH


def exchange_tokens(tok_ref, all_ref, send_sem, recv_sem):
    dp = lax.axis_index("dp")
    barrier = pltpu.get_barrier_semaphore()
    for i in range(1, 16):
        pl.semaphore_signal(
            barrier, inc=1, device_id={"dp": (dp + i) % 16}, device_id_type=MESH
        )
    pl.semaphore_wait(barrier, 15)
    copies = []
    for i in range(1, 16):
        copy = pltpu.make_async_remote_copy(
            src_ref=tok_ref,
            dst_ref=all_ref.at[dp],
            send_sem=send_sem.at[i],
            recv_sem=recv_sem,
            device_id={"dp": (dp + i) % 16},
            device_id_type=MESH,
        )
        copy.start()
        copies.append(copy)
    pltpu.make_async_copy(tok_ref, all_ref.at[dp], recv_sem).start()
    pltpu.make_async_copy(all_ref, all_ref, recv_sem).wait()
    for copy in copies:
        copy.wait_send()


def look_up(toks, table_ref, gain_ref, found_ref):
    lane = lax.broadcasted_iota(jnp.int32, (16, 128), 1)
    gain_tail = jnp.where(lane == NROWS - 128, gain_ref[...], 0.0)

    def entry(e, carry):
        for s in (0, 1):
            d2 = ((e // 2) * 2 + s) * 2 + e % 2
            for half, count in ((0, 128), (1, NROWS - 128)):

                def one(n, held):
                    token = toks[d2, half, n]
                    block = lax.shift_right_logical(token, 7)
                    offset = jnp.bitwise_and(token, 127)
                    tile = table_ref[:, pl.ds(pl.multiple_of(block * 128, 128), 128)]
                    turned = pltpu.roll(
                        tile.astype(F32), jnp.bitwise_and(n + 128 - offset, 127), 1
                    )
                    return jnp.where(lane == n, turned, held)

                start = jnp.zeros((16, 128), F32) if half == 0 else gain_tail
                found = lax.fori_loop(0, count, one, start, unroll=16)
                found_ref[e, s, :, pl.ds(half * 128, 128)] = found.astype(BF)
        return carry

    lax.fori_loop(0, 8, entry, 0)


def kernel(
    found_ref,
    ws_ref,
    wo_ref,
    cache_ref,
    cos_ref,
    sin_ref,
    len_ref,
    out_ref,
    lrecv,
    xt,
    xb,
    res,
    wbuf,
    wobuf,
    cbuf,
    qsend,
    qrecv,
    asend,
    arecv,
    att,
    qacc,
    kvacc,
    ssq,
    acc,
    sbuf,
    rright,
    rleft,
    frecv,
    send_sem,
    l_sem,
    x_sem,
    res_sem,
    w_sem,
    wo_sem,
    c_sem,
    q_sem,
    a_sem,
    rr_sem,
    rl_sem,
    f_sem,
):
    dp = lax.axis_index("dp")
    tn = lax.axis_index("tensor")
    x = dp // 4
    yh = (dp // 2) % 2
    c = dp % 2
    z = tn // 4
    b = tn % 4
    zpar = z % 2
    match = zpar == yh
    pair = b // 2
    bset = b % 2

    def dev(dp_, tn_):
        return {"dp": dp_, "tensor": tn_}

    def dpi(x_, yh_, c_):
        return (x_ * 2 + yh_) * 2 + c_

    pending = []
    counter = [0]

    def remote(src, dst, rsem, where, cond=None):
        n = counter[0]
        counter[0] += 1
        copy = pltpu.make_async_remote_copy(
            src_ref=src,
            dst_ref=dst,
            send_sem=send_sem.at[n],
            recv_sem=rsem,
            device_id=where,
            device_id_type=MESH,
        )
        if cond is None:
            copy.start()
        else:
            pl.when(cond)(copy.start)
        pending.append((cond, copy))

    def local(src, dst, sem, cond=None):
        copy = pltpu.make_async_copy(src, dst, sem)
        if cond is None:
            copy.start()
        else:
            pl.when(cond)(copy.start)

    def arrived(dst, sem):
        pltpu.make_async_copy(dst, dst, sem).wait()

    def to(src, dst, rsem, dp_, tn_):
        here = jnp.logical_and(dp_ == dp, tn_ == tn)
        remote(src, dst, rsem, dev(dp_, tn_), jnp.logical_not(here))
        local(src, dst, rsem, here)

    xr = (x + 1) % NX
    xl = (x + NX - 1) % NX
    xo = (x + 2) % NX
    zr = (z + 1) % NZ
    zl = (z + NZ - 1) % NZ
    right_z = dev(dp, zr * NB + b)
    left_z = dev(dp, zl * NB + b)

    barrier = pltpu.get_barrier_semaphore()
    partners = 0
    for i in range(1, 16):
        pl.semaphore_signal(barrier, inc=1, device_id=dev((dp + i) % 16, tn), device_id_type=MESH)
        partners += 1
    for i in range(1, 8):
        if i == 4:
            continue
        u = (yh * 4 + b + i) % 8
        pl.semaphore_signal(
            barrier, inc=1, device_id=dev(dpi(x, u // 4, c), z * NB + u % 4), device_id_type=MESH
        )
        partners += 1
    for where in (right_z, left_z):
        pl.semaphore_signal(barrier, inc=1, device_id=where, device_id_type=MESH)
        partners += 1
    pl.semaphore_wait(barrier, partners)

    for e in range(8):
        to(found_ref.at[e], lrecv.at[dp], l_sem, dpi(e // 2, zpar, e % 2), tn)

    class Gather:
        def __init__(self, src, buf, sem, half):
            self.src, self.buf, self.sem, self.half = src, buf, sem, half

        def slot(self, q, x_, c_, h=None):
            ref = self.buf.at[q, x_, c_]
            if h is None:
                return ref
            return ref.at[pl.ds(h * self.half, self.half)]

        def s(self, q, x_, c_, h=0):
            return self.sem.at[((q * NX + x_) * 2 + c_) * 2 + h]

        def send(self, src, q, x_, where):
            remote(src, self.slot(q, x_, c), self.s(q, x_, c), where)

        def first(self):
            own = (bset, x)
            local(self.src, self.slot(*own, c), self.s(*own, c))
            self.send(self.src, *own, dev(dp, z * NB + pair * 2 + 1 - bset))
            self.send(self.src, *own, dev(dpi(xr, yh, c), tn))
            self.send(self.src, *own, dev(dpi(xl, yh, c), tn))
            self.send(self.src, *own, dev(dpi(x, yh, 1 - c), tn))

        def second(self):
            q = 1 - bset
            arrived(self.slot(q, x, c), self.s(q, x, c))
            src = self.slot(q, x, c)
            self.send(src, q, x, dev(dpi(xr, yh, c), tn))
            self.send(src, q, x, dev(dpi(xl, yh, c), tn))
            self.send(src, q, x, dev(dpi(x, yh, 1 - c), tn))

        def relay(self, q):
            for x_, h, to_x in ((xl, 0, xr), (xr, 1, xl)):
                arrived(self.slot(q, x_, c), self.s(q, x_, c))
                remote(
                    self.slot(q, x_, c, h),
                    self.slot(q, x_, c, h),
                    self.s(q, x_, c, h),
                    dev(dpi(to_x, yh, c), tn),
                )
                self.send(self.slot(q, x_, c), q, x_, dev(dpi(x, yh, 1 - c), tn))

        def last(self, q):
            for h in (0, 1):
                arrived(self.slot(q, xo, c, h), self.s(q, xo, c, h))
            self.send(self.slot(q, xo, c), q, xo, dev(dpi(x, yh, 1 - c), tn))

        def finish(self):
            arrived(self.slot(bset, x, c), self.s(bset, x, c))
            for q in (0, 1):
                for x_ in range(NX):
                    arrived(self.slot(q, x_, 1 - c), self.s(q, x_, 1 - c))

    wqkv = Gather(ws_ref, wbuf, w_sem, 320)
    wout = Gather(wo_ref, wobuf, wo_sem, 128)
    wqkv.first()

    for i in range(NB):
        b2 = (b + i) % NB
        to(cache_ref.at[pl.ds(b2 * 10, 10)], cbuf.at[b], c_sem, dp, z * NB + b2)

    wqkv.second()
    wqkv.relay(bset)

    k_here = z // 2

    @pl.when(match)
    def _():
        arrived(lrecv, l_sem)
        for s in (0, 1):
            features = lrecv[:, s].reshape(256, 256).astype(F32)
            xt[s] = features.T[:XROWS].astype(BF)

    for s in (0, 1):
        for h in (0, 1):
            b2 = s + 2 * h
            same = b2 == b
            remote(
                xt.at[s],
                xb.at[k_here, b],
                x_sem.at[k_here * NB + b],
                dev(dp, z * NB + b2),
                jnp.logical_and(match, jnp.logical_not(same)),
            )
            local(
                xt.at[s], xb.at[k_here, b], x_sem.at[k_here * NB + b], jnp.logical_and(match, same)
            )

    def gather_z(j):
        delta = jnp.where(match, (0, 2, 6, 4)[j], (1, 7, 3, 5)[j])
        k = ((z - delta + NZ) % NZ) // 2
        for b_ in range(NB):
            reach = 4 if b_ < 2 else 3
            block = xb.at[k, b_]
            sem = x_sem.at[k * NB + b_]
            arrived(block, sem)
            if j < 3:
                remote(block, block, sem, right_z, delta < reach)
                remote(
                    block,
                    block,
                    sem,
                    left_z,
                    jnp.logical_or(
                        delta == 0, jnp.logical_and(delta > reach, 8 - delta < 7 - reach)
                    ),
                )
            else:
                remote(block, block, sem, right_z, delta < reach)
                remote(
                    block,
                    block,
                    sem,
                    left_z,
                    jnp.logical_and(delta > reach, 8 - delta < 7 - reach),
                )
        return k

    def project(k, start):
        for b_ in range(NB):
            raw = xb[k, b_].astype(F32)
            rows = raw[:NROWS]
            gain = raw[NROWS : NROWS + 1]
            scaled = (rows * gain).astype(BF)
            square = rows * rows
            square = square[:, :128] + square[:, 128:]
            c_ = b_ // 2
            h = b_ % 2
            parts = [
                jnp.dot(
                    scaled, wbuf[q, k, c_, h * 256 : h * 256 + 256], preferred_element_type=F32
                )
                for q in (0, 1)
            ]
            keyval = jnp.concatenate(
                [wbuf[q, k, c_, 512 + h * 64 : 576 + h * 64] for q in (0, 1)], axis=0
            )
            kv = lax.dot_general(
                scaled, keyval, (((1,), (1,)), ((), ())), preferred_element_type=F32
            )
            if start and b_ == 0:
                ssq[...] = square
                qacc[:, :256] = parts[0]
                qacc[:, 256:] = parts[1]
                kvacc[...] = kv
            else:
                ssq[...] += square
                qacc[:, :256] += parts[0]
                qacc[:, 256:] += parts[1]
                kvacc[...] += kv

    ks = [gather_z(0)]
    wqkv.relay(1 - bset)
    ks.append(gather_z(1))
    wqkv.last(bset)
    wqkv.last(1 - bset)
    wout.first()
    wqkv.finish()
    project(ks[0], True)
    ks.append(gather_z(2))
    project(ks[1], False)
    project(ks[2], False)
    ks.append(gather_z(3))
    project(ks[3], False)

    for_partner = 1 - zpar
    remote(xt.at[for_partner], res, res_sem, dev(dpi(x, for_partner, c), tn), match)
    local(xt.at[yh], res, res_sem, match)

    row40 = lax.broadcasted_iota(jnp.int32, (QROWS, 128), 0)
    lane40 = lax.broadcasted_iota(jnp.int32, (QROWS, 128), 1)
    diagonal = row40 == lane40
    row8 = lax.broadcasted_iota(jnp.int32, (8, 128), 0)
    for i in range(NB):
        total = jnp.sum(ssq[i * QROWS : (i + 1) * QROWS], axis=1, keepdims=True)
        flat = jnp.sum(jnp.where(diagonal, total, 0.0), axis=0, keepdims=True)
        high = flat.astype(BF).astype(F32)
        low = flat - high
        tail = jnp.where(row8 == 0, high, jnp.where(row8 == 1, low, 0.0))
        tail = jnp.concatenate([tail, jnp.zeros((8, 512), F32)], axis=1)
        body_rows = jnp.concatenate(
            [qacc[i * QROWS : (i + 1) * QROWS], kvacc[i * QROWS : (i + 1) * QROWS]], axis=1
        )
        qsend[i] = jnp.concatenate([body_rows, tail], axis=0).astype(BF)
        to(
            qsend.at[i],
            qrecv.at[yh, pair],
            q_sem.at[yh * 2 + pair],
            dpi(x, bset, c),
            z * NB + i,
        )

    wout.second()
    wout.relay(bset)

    for i in range(NB):
        arrived(qrecv.at[i // 2, i % 2], q_sem.at[i])
    arrived(cbuf, c_sem)

    tails = qrecv[0, 0, 32:QPAD, :128].astype(F32) + qrecv[1, 0, 32:QPAD, :128].astype(F32)
    flat = tails[8:9] + tails[9:10]
    total = jnp.sum(jnp.where(diagonal, flat, 0.0), axis=1, keepdims=True)
    factor = lax.rsqrt(total * (1.0 / FULL) + EPS)
    cosine = cos_ref[...]
    sine = sin_ref[...]

    def rope(u):
        return u * cosine + pltpu.roll(u, HEAD // 2, 1) * sine

    heads = []
    news = []
    for p in (0, 1):
        both = qrecv[0, p].astype(F32) + qrecv[1, p].astype(F32)
        both = both[:QROWS] * factor
        for i in range(4):
            heads.append(rope(both[:, i * HEAD : (i + 1) * HEAD]))
        news.append(both[:, 512:640])
    query = jnp.concatenate(heads, axis=0).astype(BF)
    no_rows = jnp.zeros((128 - QROWS, HEAD), F32)
    key_new = rope(news[0].astype(BF).astype(F32))
    key_new = jnp.concatenate([key_new, no_rows], axis=0).astype(BF)
    value_new = jnp.concatenate([news[1], no_rows], axis=0).astype(BF)
    keys = cbuf[:, :, :, :HEAD].reshape(640, HEAD)
    values = cbuf[:, :, :, HEAD:].reshape(640, HEAD)

    contract_last = (((1,), (1,)), ((), ()))
    inv_root = 1.0 / math.sqrt(HEAD)
    scores_old = lax.dot_general(query, keys, contract_last, preferred_element_type=F32) * inv_root
    scores_new = (
        lax.dot_general(query, key_new, contract_last, preferred_element_type=F32) * inv_root
    )
    col = lax.broadcasted_iota(jnp.int32, (QROWS, 640), 1)
    row = lax.broadcasted_iota(jnp.int32, (QROWS, 640), 0) // 4
    within = col % 160
    position = (col // 160) * 16 + within % 16
    old_ok = jnp.logical_and(within // 16 == row, position < len_ref[:, :1])
    new_ok = jnp.logical_and(
        lane40 // 4 == row40 // 4, jnp.logical_and(lane40 <= row40, lane40 < QROWS)
    )
    old_bias = jnp.where(old_ok, 0.0, -1e30)
    new_bias = jnp.where(new_ok, 0.0, -1e30)
    old_bias = jnp.concatenate([old_bias] * 8, axis=0)
    new_bias = jnp.concatenate([new_bias] * 8, axis=0)
    scores_old = jnp.where(old_bias == 0.0, scores_old, -1e30)
    scores_new = jnp.where(new_bias == 0.0, scores_new, -1e30)
    top = jnp.maximum(
        jnp.max(scores_old, axis=1, keepdims=True), jnp.max(scores_new, axis=1, keepdims=True)
    )
    exp_old = jnp.exp(scores_old - top)
    exp_new = jnp.exp(scores_new - top)
    totals = jnp.sum(exp_old, axis=1, keepdims=True) + jnp.sum(exp_new, axis=1, keepdims=True)
    probs_old = (exp_old / totals).astype(BF)
    probs_new = (exp_new / totals).astype(BF)
    attended = jnp.dot(probs_old, values, preferred_element_type=F32)
    attended = attended + jnp.dot(probs_new, value_new, preferred_element_type=F32)
    for p in (0, 1):
        side = jnp.concatenate(
            [attended[(4 * p + i) * QROWS : (4 * p + i + 1) * QROWS] for i in range(4)], axis=1
        )
        asend[p] = jnp.concatenate([side, jnp.zeros((QPAD - QROWS, 512), F32)], axis=0).astype(BF)
        for y_ in (0, 1):
            to(asend.at[p], arecv.at[b], a_sem.at[b], dpi(x, y_, c), z * NB + p * 2 + yh)

    wout.relay(1 - bset)
    wout.last(bset)
    wout.last(1 - bset)
    wout.finish()
    for i in range(NB):
        arrived(arecv.at[i], a_sem.at[i])
    att[...] = jnp.concatenate(
        [arecv[i].astype(F32)[:QROWS] for i in range(NB)], axis=0
    ).astype(BF)

    for j in range(4):
        delta = jnp.where(match, (4, 2, 6, 0)[j], (3, 5, 1, 7)[j])
        k = ((z + delta) % NZ) // 2
        is_end = delta == 0
        for b_ in range(NB):
            reach = 4 if b_ < 2 else 3
            c_ = b_ // 2
            h = b_ % 2
            part = jnp.dot(
                att[:, :256],
                wobuf[0, k, c_, :, h * 256 : h * 256 + 256],
                preferred_element_type=F32,
            )
            part = part + jnp.dot(
                att[:, 256:],
                wobuf[1, k, c_, :, h * 256 : h * 256 + 256],
                preferred_element_type=F32,
            )
            acc[...] = part
            go_right = jnp.logical_and(delta >= 1, delta <= reach)
            go_left = delta > reach
            from_left = delta + 1 <= reach
            from_right = jnp.logical_or(delta > reach + 1, is_end)
            index = k * NB + b_

            @pl.when(from_left)
            def _(index=index, k=k, b_=b_):
                arrived(rright.at[k, b_], rr_sem.at[index])
                acc[...] += rright[k, b_].astype(F32)

            @pl.when(from_right)
            def _(index=index, k=k, b_=b_):
                arrived(rleft.at[k, b_], rl_sem.at[index])
                acc[...] += rleft[k, b_].astype(F32)

            sbuf[k, b_] = acc[...].astype(BF)
            remote(sbuf.at[k, b_], rright.at[k, b_], rr_sem.at[index], right_z, go_right)
            remote(sbuf.at[k, b_], rleft.at[k, b_], rl_sem.at[index], left_z, go_left)
            if j == 3:
                dp_ = dpi(x, bset, c)
                tn_ = z * NB + b_
                here = jnp.logical_and(dp_ == dp, tn_ == tn)
                remote(
                    sbuf.at[k, b_],
                    frecv.at[pair],
                    f_sem.at[pair],
                    dev(dp_, tn_),
                    jnp.logical_and(is_end, jnp.logical_not(here)),
                )
                local(
                    sbuf.at[k, b_],
                    frecv.at[pair],
                    f_sem.at[pair],
                    jnp.logical_and(is_end, here),
                )

    arrived(res, res_sem)
    for p in (0, 1):
        arrived(frecv.at[p], f_sem.at[p])
    out_ref[...] = (
        res[:NROWS].astype(F32) + (frecv[0].astype(F32) + frecv[1].astype(F32))
    ).astype(BF)

    for cond, copy in pending:
        if cond is None:
            copy.wait_send()
        else:
            pl.when(cond)(copy.wait_send)


def body(
    token_ids, lengths, embed_table, norm_gain, w_query, key_value_weight, w_out, key_value_cache
):
    dp = lax.axis_index("dp")
    quarter = lax.axis_index("tensor") % NB
    tokens = jnp.pad(token_ids.T.reshape(-1), (0, 1024 - NROWS)).reshape(8, 128)
    table = embed_table.reshape(16, -1)
    gain = lax.dynamic_slice(norm_gain, (dp * 16,), (16,)).astype(F32)
    gain = jnp.broadcast_to(gain[:, None], (16, 128))
    keyval = key_value_weight.T.reshape(64, 2, 256).transpose(1, 0, 2).reshape(128, 256)
    shard = jnp.concatenate([w_query, keyval], axis=0)
    cache = key_value_cache.reshape(40, 16, 256)
    here = jnp.repeat(lax.dynamic_slice(lengths, (quarter * 10,), (10,)), 4)
    position = here + jnp.tile(jnp.arange(4, dtype=jnp.int32), 10)
    frequency = THETA ** (-(jnp.arange(64, dtype=F32) / 64))
    turn = position.astype(F32)[:, None] * frequency
    cosine = jnp.cos(turn)
    sine = jnp.sin(turn)
    cosine = jnp.concatenate([cosine, cosine], axis=1)
    sine = jnp.concatenate([-sine, sine], axis=1)
    lens = jnp.broadcast_to(here[:, None], (QROWS, 128))

    vmem = pl.BlockSpec(memory_space=pltpu.VMEM)
    anywhere = pl.BlockSpec(memory_space=pl.ANY)
    dma = pltpu.SemaphoreType.DMA
    all_tokens = pl.pallas_call(
        exchange_tokens,
        out_shape=jax.ShapeDtypeStruct((16, 8, 128), jnp.int32),
        in_specs=[vmem],
        out_specs=vmem,
        scratch_shapes=[dma((16,)), dma],
        compiler_params=pltpu.CompilerParams(collective_id=1, has_side_effects=True),
        name="exchange_tokens",
    )(tokens)
    found = pl.pallas_call(
        look_up,
        out_shape=jax.ShapeDtypeStruct((8, 2, 16, 256), BF),
        in_specs=[pl.BlockSpec(memory_space=pltpu.SMEM), vmem, vmem],
        out_specs=vmem,
        compiler_params=pltpu.CompilerParams(vmem_limit_bytes=16 * 1024 * 1024),
        name="look_up",
    )(all_tokens, table, gain)
    out = pl.pallas_call(
        kernel,
        out_shape=jax.ShapeDtypeStruct((NROWS, 256), BF),
        in_specs=[anywhere, anywhere, anywhere, anywhere, vmem, vmem, vmem],
        out_specs=vmem,
        scratch_shapes=[
            pltpu.VMEM((16, 2, 16, 256), BF),
            pltpu.VMEM((2, XROWS, 256), BF),
            pltpu.VMEM((4, NB, XROWS, 256), BF),
            pltpu.VMEM((XROWS, 256), BF),
            pltpu.VMEM((2, NX, 2, 640, 256), BF),
            pltpu.VMEM((2, NX, 2, 256, 512), BF),
            pltpu.VMEM((NB, 10, 16, 256), BF),
            pltpu.VMEM((NB, QPAD, 640), BF),
            pltpu.VMEM((2, 2, QPAD, 640), BF),
            pltpu.VMEM((2, QPAD, 512), BF),
            pltpu.VMEM((NB, QPAD, 512), BF),
            pltpu.VMEM((NROWS, 512), BF),
            pltpu.VMEM((NROWS, 512), F32),
            pltpu.VMEM((NROWS, 128), F32),
            pltpu.VMEM((NROWS, 128), F32),
            pltpu.VMEM((NROWS, 256), F32),
            pltpu.VMEM((4, NB, NROWS, 256), BF),
            pltpu.VMEM((4, NB, NROWS, 256), BF),
            pltpu.VMEM((4, NB, NROWS, 256), BF),
            pltpu.VMEM((2, NROWS, 256), BF),
            dma((192,)),
            dma,
            dma((16,)),
            dma,
            dma((32,)),
            dma((32,)),
            dma,
            dma((4,)),
            dma((4,)),
            dma((16,)),
            dma((16,)),
            dma((2,)),
        ],
        compiler_params=pltpu.CompilerParams(
            collective_id=0, has_side_effects=True, vmem_limit_bytes=56 * 1024 * 1024
        ),
        name="decode_block",
    )(found, shard, w_out, cache, cosine, sine, lens)
    return out.reshape(40, 4, 256).transpose(1, 0, 2)


def solution(mesh):
    in_specs = (
        P(None, "dp"),
        P("dp"),
        P(None, "tensor", "dp", None),
        P("tensor"),
        P("dp", "tensor"),
        P("dp", "tensor"),
        P("tensor", "dp"),
        P("dp", "tensor", None, None),
    )
    out_specs = P(None, "dp", "tensor")
    return jax.shard_map(body, mesh=mesh, in_specs=in_specs, out_specs=out_specs, check_vma=False)
```

time: 648 us -> 170 us (0.26)
  the two profiles are of different devices: /device:TPU:2 before, /device:TPU:56 now
where the time goes in v1:
time: 170 us; the launch traced here: 169 us
  Pallas kernels  159 us (94%)
  local copies, waits for them, and re-layouts  7.98 us (5%)
  other arithmetic  2.4 us (1%)
    pallas_call x1, Pallas kernels, body(): pl.pallas_call(kernel, out_shape=jax.ShapeDtypeStruct((NROWS, 256), BF),...  123 us
    pallas_call x1, Pallas kernels, body(): pl.pallas_call(look_up, out_shape=jax.ShapeDtypeStruct((8, 2, 16, 256), B...  22.8 us
    pallas_call x1, Pallas kernels, body(): pl.pallas_call(exchange_tokens, out_shape=jax.ShapeDtypeStruct((16, 8, 12...  13.5 us

profile of v1, /device:TPU:56, one launch (start us, length us, event | category | flops | bytes accessed | tf_op | source)
XLA Modules:
  0.0 169.4 jit_solution(5110371396617041016)
XLA Ops:
  0.0 0.0 copy-start.4
  0.0 0.0 copy-start.3
  0.0 0.8 dynamic-slice_convert_fusion
  0.8 0.7 dynamic_slice.7
  1.5 0.1 broadcast_in_dim.7
  1.6 0.1 reshape.48
  1.7 0.1 broadcast_in_dim.6.gain_ref
  1.7 0.1 tile.10
  1.8 0.7 broadcast_in_dim.8.len_ref
  2.5 0.8 copy.11
  3.3 0.1 reshape.42
  3.4 0.6 pad_bitcast_fusion.tok_ref
  4.0 0.2 fusion
  4.1 0.7 pad_maximum_fusion.1
  4.8 13.5 %exchange_tokens.1.toks = s32[16,8,128]{2,1,0:T(8,128)} custom-call(s32[8,128]{1,0:T(8,128)} %pad_bitcast_fusion.tok_ref), custom_call_target="tpu_custom_call" | custom-call | tf_op jit(solution)/shard_map/exchange_tokens/pallas_call | solution.py:575
  18.3 0.0 copy-start
  18.3 1.7 %copy-done = bf16[16,1,1,81920]{3,0,2,1:T(8,128)(2,1)S(1)} copy-done((bf16[16,1,1,81920]{3,0,2,1:T(8,128)(2,1)S(1)}, bf16[16,1,1,81920]{3,0,2,1:T(8,128)(2,1)}, u32[]{:S(2)}) %copy-start) | copy-done | bytes 2621464
  20.1 0.0 copy-start.2
  20.1 0.8 copy-done.2
  20.9 22.8 %look_up.1.found_ref = bf16[8,2,16,256]{3,2,1,0:T(8,128)(2,1)S(1)} custom-call(s32[16,8,128]{2,1,0:T(8,128)S(1)} %copy-done.2, bf16[16,81920]{1,0:T(8,128)(2,1)S(1)} %bitcast.16, f32[16,128]{1,0:T(8,128)S(1)} %broadcast_in_dim.6.gain_ref), custom_call_target="tpu_custom_call" | custom-call | tf_op jit(solution)/shard_map/look_up/pallas_call | solution.py:584
  43.7 0.0 copy-start.1
  43.7 0.7 copy-done.1
  44.3 0.0 copy-done.4
  44.3 0.0 copy-done.3
  44.3 0.8 pad_maximum_fusion.ws_ref
  45.1 122.8 %decode_block.1 = bf16[160,256]{1,0:T(8,128)(2,1)} custom-call(bf16[8,2,16,256]{3,2,1,0:T(8,128)(2,1)} %copy-done.1, bf16[640,256]{1,0:T(8,128)(2,1)} %pad_maximum_fusion.ws_ref, bf16[256,512]{1,0:T(8,128)(2,1)} %wo_ref.1, bf16[40,16,256]{2,1,0:T(8,128)(2,1)} %bitcast.17, f32[40,128]{1,0:T(8,128)} %get-tuple-element.8.cos_ref, ...), custom_call_target="tpu_custom_call" | custom-call | tf_op jit(solution)/shard_map/decode_block/pallas_call | solution.py:592
  167.9 0.9 reshape.49
  168.8 0.6 copy.17
  (4 shorter events, 0.0 us)
Async XLA Ops:
  0.0 44.3 %copy-start.4 = (bf16[512,64]{0,1:T(8,128)(2,1)S(1)}, bf16[512,64]{0,1:T(8,128)(2,1)}, u32[]{:S(2)}) copy-start(bf16[512,64]{0,1:T(8,128)(2,1)} %param.13) | copy-start | bytes 196612
  0.0 44.3 %copy-start.3 = (bf16[512,256]{1,0:T(8,128)(2,1)S(1)}, bf16[512,256]{1,0:T(8,128)(2,1)}, u32[]{:S(2)}) copy-start(bf16[512,256]{1,0:T(8,128)(2,1)} %param.12) | copy-start | bytes 786436
  18.3 1.7 %copy-start = (bf16[16,1,1,81920]{3,0,2,1:T(8,128)(2,1)S(1)}, bf16[16,1,1,81920]{3,0,2,1:T(8,128)(2,1)}, u32[]{:S(2)}) copy-start(bf16[16,1,1,81920]{3,0,2,1:T(8,128)(2,1)} %param.10) | copy-start | bytes 7864324
  20.1 0.8 copy-start.2
  43.7 0.7 copy-start.1

commit v2 on v1

--- a/solution.py
+++ b/solution.py
@@ -3,6 +3,7 @@
 
 import jax
 import jax.numpy as jnp
+import numpy as np
 from jax import lax
 from jax.experimental import pallas as pl
 from jax.experimental.pallas import tpu as pltpu
@@ -26,68 +27,22 @@
 MESH = pl.DeviceIdType.MESH
 
 
-def exchange_tokens(tok_ref, all_ref, send_sem, recv_sem):
-    dp = lax.axis_index("dp")
-    barrier = pltpu.get_barrier_semaphore()
-    for i in range(1, 16):
-        pl.semaphore_signal(
-            barrier, inc=1, device_id={"dp": (dp + i) % 16}, device_id_type=MESH
-        )
-    pl.semaphore_wait(barrier, 15)
-    copies = []
-    for i in range(1, 16):
-        copy = pltpu.make_async_remote_copy(
-            src_ref=tok_ref,
-            dst_ref=all_ref.at[dp],
-            send_sem=send_sem.at[i],
-            recv_sem=recv_sem,
-            device_id={"dp": (dp + i) % 16},
-            device_id_type=MESH,
-        )
-        copy.start()
-        copies.append(copy)
-    pltpu.make_async_copy(tok_ref, all_ref.at[dp], recv_sem).start()
-    pltpu.make_async_copy(all_ref, all_ref, recv_sem).wait()
-    for copy in copies:
-        copy.wait_send()
-
-
-def look_up(toks, table_ref, gain_ref, found_ref):
-    lane = lax.broadcasted_iota(jnp.int32, (16, 128), 1)
-    gain_tail = jnp.where(lane == NROWS - 128, gain_ref[...], 0.0)
-
-    def entry(e, carry):
-        for s in (0, 1):
-            d2 = ((e // 2) * 2 + s) * 2 + e % 2
-            for half, count in ((0, 128), (1, NROWS - 128)):
-
-                def one(n, held):
-                    token = toks[d2, half, n]
-                    block = lax.shift_right_logical(token, 7)
-                    offset = jnp.bitwise_and(token, 127)
-                    tile = table_ref[:, pl.ds(pl.multiple_of(block * 128, 128), 128)]
-                    turned = pltpu.roll(
-                        tile.astype(F32), jnp.bitwise_and(n + 128 - offset, 127), 1
-                    )
-                    return jnp.where(lane == n, turned, held)
-
-                start = jnp.zeros((16, 128), F32) if half == 0 else gain_tail
-                found = lax.fori_loop(0, count, one, start, unroll=16)
-                found_ref[e, s, :, pl.ds(half * 128, 128)] = found.astype(BF)
-        return carry
-
-    lax.fori_loop(0, 8, entry, 0)
-
-
 def kernel(
-    found_ref,
-    ws_ref,
+    tok_ref,
+    table_ref,
+    gain_ref,
+    freq_ref,
+    wq_ref,
+    wkv_ref,
     wo_ref,
     cache_ref,
+    out_ref,
+    tab,
+    tokv,
+    toks,
+    lsend,
     cos_ref,
     sin_ref,
-    len_ref,
-    out_ref,
     lrecv,
     xt,
     xb,
@@ -109,6 +64,8 @@
     rleft,
     frecv,
     send_sem,
+    loc_sem,
+    tok_sem,
     l_sem,
     x_sem,
     res_sem,
@@ -182,6 +139,16 @@
     right_z = dev(dp, zr * NB + b)
     left_z = dev(dp, zl * NB + b)
 
+    table_copy = pltpu.make_async_copy(table_ref, tab, loc_sem.at[0])
+    table_copy.start()
+    own_shard = wbuf.at[bset, x, c]
+    own_sem = w_sem.at[((bset * NX + x) * 2 + c) * 2]
+    local(wq_ref, own_shard.at[pl.ds(0, 512)], own_sem)
+    for h in (0, 1):
+        local(
+            wkv_ref.at[:, pl.ds(h * 256, 256)], own_shard.at[pl.ds(512 + h * 64, 64)], own_sem
+        )
+
     barrier = pltpu.get_barrier_semaphore()
     partners = 0
     for i in range(1, 16):
@@ -198,14 +165,26 @@
     for where in (right_z, left_z):
         pl.semaphore_signal(barrier, inc=1, device_id=where, device_id_type=MESH)
         partners += 1
+
+    row40 = lax.broadcasted_iota(jnp.int32, (QROWS, 128), 0)
+    lane40 = lax.broadcasted_iota(jnp.int32, (QROWS, 128), 1)
+    lengths = tok_ref[4:5].astype(F32)
+    length = jnp.sum(
+        jnp.where(lane40 == b * 10 + row40 // 4, lengths, 0.0), axis=1, keepdims=True
+    )
+    turn = (length + (row40 % 4).astype(F32)) * freq_ref[...]
+    cos_ref[...] = jnp.cos(turn)
+    sin_ref[...] = jnp.where(lane40 < HEAD // 2, -1.0, 1.0) * jnp.sin(turn)
+
     pl.semaphore_wait(barrier, partners)
 
-    for e in range(8):
-        to(found_ref.at[e], lrecv.at[dp], l_sem, dpi(e // 2, zpar, e % 2), tn)
+    for i in range(1, 16):
+        remote(tok_ref, tokv.at[dp], tok_sem, dev((dp + i) % 16, tn))
+    local(tok_ref, tokv.at[dp], tok_sem)
 
     class Gather:
-        def __init__(self, src, buf, sem, half):
-            self.src, self.buf, self.sem, self.half = src, buf, sem, half
+        def __init__(self, buf, sem, half):
+            self.buf, self.sem, self.half = buf, sem, half
 
         def slot(self, q, x_, c_, h=None):
             ref = self.buf.at[q, x_, c_]
@@ -221,11 +200,12 @@
 
         def first(self):
             own = (bset, x)
-            local(self.src, self.slot(*own, c), self.s(*own, c))
-            self.send(self.src, *own, dev(dp, z * NB + pair * 2 + 1 - bset))
-            self.send(self.src, *own, dev(dpi(xr, yh, c), tn))
-            self.send(self.src, *own, dev(dpi(xl, yh, c), tn))
-            self.send(self.src, *own, dev(dpi(x, yh, 1 - c), tn))
+            src = self.slot(*own, c)
+            arrived(src, self.s(*own, c))
+            self.send(src, *own, dev(dp, z * NB + pair * 2 + 1 - bset))
+            self.send(src, *own, dev(dpi(xr, yh, c), tn))
+            self.send(src, *own, dev(dpi(xl, yh, c), tn))
+            self.send(src, *own, dev(dpi(x, yh, 1 - c), tn))
 
         def second(self):
             q = 1 - bset
@@ -252,21 +232,77 @@
             self.send(self.slot(q, xo, c), q, xo, dev(dpi(x, yh, 1 - c), tn))
 
         def finish(self):
-            arrived(self.slot(bset, x, c), self.s(bset, x, c))
             for q in (0, 1):
                 for x_ in range(NX):
                     arrived(self.slot(q, x_, 1 - c), self.s(q, x_, 1 - c))
 
-    wqkv = Gather(ws_ref, wbuf, w_sem, 320)
-    wout = Gather(wo_ref, wobuf, wo_sem, 128)
+    wqkv = Gather(wbuf, w_sem, 320)
+    wout = Gather(wobuf, wo_sem, 128)
     wqkv.first()
+    local(wo_ref, wout.slot(bset, x, c), wout.s(bset, x, c))
+
+    arrived(tokv, tok_sem)
+    to_scalar = pltpu.make_async_copy(tokv, toks, loc_sem.at[1])
+    to_scalar.start()
+    to_scalar.wait()
+    table_copy.wait()
+
+    lane = lax.broadcasted_iota(jnp.int32, (16, 128), 1)
+    wide = lax.broadcasted_iota(jnp.int32, (16, 256), 1)
+    feature = lax.broadcasted_iota(jnp.int32, (16, 256), 0)
+    gain_column = jnp.sum(
+        jnp.where(wide == dp * 16 + feature, gain_ref[...].astype(F32), 0.0),
+        axis=1,
+        keepdims=True,
+    )
+    gain_tail = jnp.where(lane == NROWS - 128, gain_column, 0.0)
+    place = x * 2 + c
+    lookup_base = counter[0]
+    counter[0] += 8
+
+    def lookup_copy(e):
+        dp2 = dpi(e // 2, zpar, e % 2)
+        return dp2, pltpu.make_async_remote_copy(
+            src_ref=lsend.at[e],
+            dst_ref=lrecv.at[dp],
+            send_sem=send_sem.at[lookup_base + e],
+            recv_sem=l_sem,
+            device_id=dev(dp2, tn),
+            device_id_type=MESH,
+        )
+
+    def lookup(i, carry):
+        e = (place + 1 + i) % 8
+
+        def one_set(s, carry):
+            d2 = dpi(e // 2, s, e % 2)
+            for half, count in ((0, 128), (1, NROWS - 128)):
+                found = jnp.zeros((16, 128), F32) if half == 0 else gain_tail
+                for n in range(count):
+                    row = half * 128 + n
+                    token = toks[d2, row % 4, row // 4]
+                    block = lax.shift_right_logical(token, 7)
+                    tile = tab[:, pl.ds(block * 128, 128)].astype(F32)
+                    picked = jnp.where(lane == jnp.bitwise_and(token, 127), tile, 0.0)
+                    found = jnp.where(lane == n, jnp.sum(picked, axis=1, keepdims=True), found)
+                lsend[e, s, :, pl.ds(half * 128, 128)] = found.astype(BF)
+            return carry
+
+        lax.fori_loop(0, 2, one_set, 0)
+        dp2, copy = lookup_copy(e)
+        pl.when(dp2 != dp)(copy.start)
+        pl.when(dp2 == dp)(pltpu.make_async_copy(lsend.at[e], lrecv.at[dp], l_sem).start)
+        return carry
+
+    lax.fori_loop(0, 4, lookup, 0)
+    wqkv.second()
+    wqkv.relay(bset)
+    lax.fori_loop(4, 8, lookup, 0)
+    wqkv.relay(1 - bset)
 
     for i in range(NB):
         b2 = (b + i) % NB
         to(cache_ref.at[pl.ds(b2 * 10, 10)], cbuf.at[b], c_sem, dp, z * NB + b2)
-
-    wqkv.second()
-    wqkv.relay(bset)
 
     k_here = z // 2
 
@@ -355,26 +391,25 @@
                 qacc[:, 256:] += parts[1]
                 kvacc[...] += kv
 
-    ks = [gather_z(0)]
-    wqkv.relay(1 - bset)
-    ks.append(gather_z(1))
     wqkv.last(bset)
     wqkv.last(1 - bset)
     wout.first()
+    ks = [gather_z(0)]
+    ks.append(gather_z(1))
     wqkv.finish()
+    wout.second()
     project(ks[0], True)
     ks.append(gather_z(2))
     project(ks[1], False)
+    wout.relay(bset)
+    ks.append(gather_z(3))
     project(ks[2], False)
-    ks.append(gather_z(3))
     project(ks[3], False)
 
     for_partner = 1 - zpar
     remote(xt.at[for_partner], res, res_sem, dev(dpi(x, for_partner, c), tn), match)
     local(xt.at[yh], res, res_sem, match)
 
-    row40 = lax.broadcasted_iota(jnp.int32, (QROWS, 128), 0)
-    lane40 = lax.broadcasted_iota(jnp.int32, (QROWS, 128), 1)
     diagonal = row40 == lane40
     row8 = lax.broadcasted_iota(jnp.int32, (8, 128), 0)
     for i in range(NB):
@@ -396,8 +431,7 @@
             z * NB + i,
         )
 
-    wout.second()
-    wout.relay(bset)
+    wout.relay(1 - bset)
 
     for i in range(NB):
         arrived(qrecv.at[i // 2, i % 2], q_sem.at[i])
@@ -439,7 +473,7 @@
     row = lax.broadcasted_iota(jnp.int32, (QROWS, 640), 0) // 4
     within = col % 160
     position = (col // 160) * 16 + within % 16
-    old_ok = jnp.logical_and(within // 16 == row, position < len_ref[:, :1])
+    old_ok = jnp.logical_and(within // 16 == row, position.astype(F32) < length)
     new_ok = jnp.logical_and(
         lane40 // 4 == row40 // 4, jnp.logical_and(lane40 <= row40, lane40 < QROWS)
     )
@@ -467,7 +501,6 @@
         for y_ in (0, 1):
             to(asend.at[p], arecv.at[b], a_sem.at[b], dpi(x, y_, c), z * NB + p * 2 + yh)
 
-    wout.relay(1 - bset)
     wout.last(bset)
     wout.last(1 - bset)
     wout.finish()
@@ -536,9 +569,12 @@
     arrived(res, res_sem)
     for p in (0, 1):
         arrived(frecv.at[p], f_sem.at[p])
-    out_ref[...] = (
-        res[:NROWS].astype(F32) + (frecv[0].astype(F32) + frecv[1].astype(F32))
-    ).astype(BF)
+    hidden = res[:NROWS].astype(F32) + (frecv[0].astype(F32) + frecv[1].astype(F32))
+    hidden = jnp.concatenate([hidden, jnp.zeros((256 - NROWS, 256), F32)], axis=0).astype(BF)
+    to_row = lax.broadcasted_iota(jnp.int32, (NROWS, 256), 0)
+    from_row = lax.broadcasted_iota(jnp.int32, (NROWS, 256), 1)
+    order = jnp.where(from_row == (to_row % 40) * 4 + to_row // 40, 1.0, 0.0).astype(BF)
+    out_ref[...] = jnp.dot(order, hidden, preferred_element_type=F32).astype(BF)
 
     for cond, copy in pending:
         if cond is None:
@@ -546,55 +582,41 @@
         else:
             pl.when(cond)(copy.wait_send)
 
+    def lookup_sent(e, carry):
+        dp2, copy = lookup_copy(e)
+        pl.when(dp2 != dp)(copy.wait_send)
+        return carry
+
+    lax.fori_loop(0, 8, lookup_sent, 0)
+
 
 def body(
     token_ids, lengths, embed_table, norm_gain, w_query, key_value_weight, w_out, key_value_cache
 ):
-    dp = lax.axis_index("dp")
-    quarter = lax.axis_index("tensor") % NB
-    tokens = jnp.pad(token_ids.T.reshape(-1), (0, 1024 - NROWS)).reshape(8, 128)
+    numbers = jnp.concatenate([token_ids, lengths[None]], axis=0)
+    numbers = jnp.pad(numbers, ((0, 3), (0, 88)))
     table = embed_table.reshape(16, -1)
-    gain = lax.dynamic_slice(norm_gain, (dp * 16,), (16,)).astype(F32)
-    gain = jnp.broadcast_to(gain[:, None], (16, 128))
-    keyval = key_value_weight.T.reshape(64, 2, 256).transpose(1, 0, 2).reshape(128, 256)
-    shard = jnp.concatenate([w_query, keyval], axis=0)
+    gain = norm_gain.reshape(1, -1)
+    frequency = THETA ** (-(np.arange(64) / 64))
+    frequency = jnp.asarray(np.concatenate([frequency, frequency])[None], F32)
+    keyval = key_value_weight.T
     cache = key_value_cache.reshape(40, 16, 256)
-    here = jnp.repeat(lax.dynamic_slice(lengths, (quarter * 10,), (10,)), 4)
-    position = here + jnp.tile(jnp.arange(4, dtype=jnp.int32), 10)
-    frequency = THETA ** (-(jnp.arange(64, dtype=F32) / 64))
-    turn = position.astype(F32)[:, None] * frequency
-    cosine = jnp.cos(turn)
-    sine = jnp.sin(turn)
-    cosine = jnp.concatenate([cosine, cosine], axis=1)
-    sine = jnp.concatenate([-sine, sine], axis=1)
-    lens = jnp.broadcast_to(here[:, None], (QROWS, 128))
 
     vmem = pl.BlockSpec(memory_space=pltpu.VMEM)
     anywhere = pl.BlockSpec(memory_space=pl.ANY)
     dma = pltpu.SemaphoreType.DMA
-    all_tokens = pl.pallas_call(
-        exchange_tokens,
-        out_shape=jax.ShapeDtypeStruct((16, 8, 128), jnp.int32),
-        in_specs=[vmem],
-        out_specs=vmem,
-        scratch_shapes=[dma((16,)), dma],
-        compiler_params=pltpu.CompilerParams(collective_id=1, has_side_effects=True),
-        name="exchange_tokens",
-    )(tokens)
-    found = pl.pallas_call(
-        look_up,
-        out_shape=jax.ShapeDtypeStruct((8, 2, 16, 256), BF),
-        in_specs=[pl.BlockSpec(memory_space=pltpu.SMEM), vmem, vmem],
-        out_specs=vmem,
-        compiler_params=pltpu.CompilerParams(vmem_limit_bytes=16 * 1024 * 1024),
-        name="look_up",
-    )(all_tokens, table, gain)
     out = pl.pallas_call(
         kernel,
         out_shape=jax.ShapeDtypeStruct((NROWS, 256), BF),
-        in_specs=[anywhere, anywhere, anywhere, anywhere, vmem, vmem, vmem],
+        in_specs=[vmem, anywhere, vmem, vmem, anywhere, anywhere, anywhere, anywhere],
         out_specs=vmem,
         scratch_shapes=[
+            pltpu.VMEM((16, 81920), BF),
+            pltpu.VMEM((16, 8, 128), jnp.int32),
+            pltpu.SMEM((16, 8, 128), jnp.int32),
+            pltpu.VMEM((8, 2, 16, 256), BF),
+            pltpu.VMEM((QROWS, HEAD), F32),
+            pltpu.VMEM((QROWS, HEAD), F32),
             pltpu.VMEM((16, 2, 16, 256), BF),
             pltpu.VMEM((2, XROWS, 256), BF),
             pltpu.VMEM((4, NB, XROWS, 256), BF),
@@ -616,6 +638,8 @@
             pltpu.VMEM((4, NB, NROWS, 256), BF),
             pltpu.VMEM((2, NROWS, 256), BF),
             dma((192,)),
+            dma((2,)),
+            dma,
             dma,
             dma((16,)),
             dma,
@@ -632,8 +656,8 @@
             collective_id=0, has_side_effects=True, vmem_limit_bytes=56 * 1024 * 1024
         ),
         name="decode_block",
-    )(found, shard, w_out, cache, cosine, sine, lens)
-    return out.reshape(40, 4, 256).transpose(1, 0, 2)
+    )(numbers, table, gain, frequency, w_query, keyval, w_out, cache)
+    return out.reshape(4, 40, 256)
 
 
 def solution(mesh):

time: 170 us -> 131 us (0.77)
  Pallas kernels: 159 us -> 126 us
  local copies, waits for them, and re-layouts: 7.98 us -> 3.33 us
    pallas_call x2 -> x0, Pallas kernels: 36.2 us -> none  [the longest x1 22.8 us: body(): pl.pallas_call(look_up, out_shape=jax.ShapeDtypeStruct((8, 2, 16, 256), B...]
    pallas_call x1, Pallas kernels: 123 us -> 126 us  [body(): pl.pallas_call(kernel, out_shape=jax.ShapeDtypeStruct((NROWS, 256), BF),...]
    unnamed x10 -> x1, local copies, waits for them, and re-layouts: 3.23 us -> 1.53 us
where the time goes in v2:
time: 131 us
  Pallas kernels  126 us (96%)
  local copies, waits for them, and re-layouts  3.33 us (3%)
    pallas_call x1, Pallas kernels, body(): pl.pallas_call(kernel, out_shape=jax.ShapeDtypeStruct((NROWS, 256), BF),...  126 us

profile of v2, /device:TPU:56, one launch (start us, length us, event | category | flops | bytes accessed | tf_op | source)
XLA Modules:
  0.0 130.5 jit_solution(4961034806239792007)
XLA Ops:
  0.0 1.2 reshape.13.gain_ref
  1.2 0.7 pad_add_fusion
  1.9 0.6 pad.4.tok_ref
  2.5 126.5 %decode_block.1 = bf16[160,256]{1,0:T(8,128)(2,1)} custom-call(s32[8,128]{1,0:T(8,128)} %pad.4.tok_ref, bf16[16,81920]{1,0:T(8,128)(2,1)} %bitcast.5, bf16[1,256]{1,0:T(2,128)(2,1)} %reshape.13.gain_ref, f32[1,128]{1,0:T(1,128)} %constant.4.clone.freq_ref, bf16[512,256]{1,0:T(8,128)(2,1)} %wq_ref.1, bf16[64,512]{1,0:T(8,128)(2,1)} %bitcast.8, ...), custom_call_target="tpu_custom_call" | custom-call | tf_op jit(solution)/shard_map/decode_block/pallas_call | solution.py:608
  129.0 1.5 %copy.11 = bf16[4,40,256]{2,1,0:T(8,128)(2,1)} copy(bf16[4,40,256]{2,1,0:T(8,128)(2,1)} %bitcast.7) | data formatting | bytes 163840

commit v3 on v2

--- a/solution.py
+++ b/solution.py
@@ -29,6 +29,7 @@
 
 def kernel(
     tok_ref,
+    len_ref,
     table_ref,
     gain_ref,
     freq_ref,
@@ -168,10 +169,10 @@
 
     row40 = lax.broadcasted_iota(jnp.int32, (QROWS, 128), 0)
     lane40 = lax.broadcasted_iota(jnp.int32, (QROWS, 128), 1)
-    lengths = tok_ref[4:5].astype(F32)
-    length = jnp.sum(
-        jnp.where(lane40 == b * 10 + row40 // 4, lengths, 0.0), axis=1, keepdims=True
-    )
+    lengths = len_ref[...].astype(F32)
+    row_of = lax.broadcasted_iota(jnp.int32, (QROWS, 40), 0) // 4 + b * 10
+    all_rows = lax.broadcasted_iota(jnp.int32, (QROWS, 40), 1)
+    length = jnp.sum(jnp.where(all_rows == row_of, lengths, 0.0), axis=1, keepdims=True)
     turn = (length + (row40 % 4).astype(F32)) * freq_ref[...]
     cos_ref[...] = jnp.cos(turn)
     sin_ref[...] = jnp.where(lane40 < HEAD // 2, -1.0, 1.0) * jnp.sin(turn)
@@ -300,115 +301,117 @@
     lax.fori_loop(4, 8, lookup, 0)
     wqkv.relay(1 - bset)
 
-    for i in range(NB):
-        b2 = (b + i) % NB
-        to(cache_ref.at[pl.ds(b2 * 10, 10)], cbuf.at[b], c_sem, dp, z * NB + b2)
-
     k_here = z // 2
 
-    @pl.when(match)
-    def _():
-        arrived(lrecv, l_sem)
-        for s in (0, 1):
+    pl.when(match)(lambda: arrived(lrecv, l_sem))
+    for s in (0, 1):
+
+        @pl.when(match)
+        def _(s=s):
             features = lrecv[:, s].reshape(256, 256).astype(F32)
             xt[s] = features.T[:XROWS].astype(BF)
 
-    for s in (0, 1):
         for h in (0, 1):
             b2 = s + 2 * h
-            same = b2 == b
+            here = b2 == b
+            dst = xb.at[k_here, b]
+            sem = x_sem.at[k_here * NB + b]
             remote(
                 xt.at[s],
-                xb.at[k_here, b],
-                x_sem.at[k_here * NB + b],
+                dst,
+                sem,
                 dev(dp, z * NB + b2),
-                jnp.logical_and(match, jnp.logical_not(same)),
+                jnp.logical_and(match, jnp.logical_not(here)),
             )
-            local(
-                xt.at[s], xb.at[k_here, b], x_sem.at[k_here * NB + b], jnp.logical_and(match, same)
-            )
-
-    def gather_z(j):
-        delta = jnp.where(match, (0, 2, 6, 4)[j], (1, 7, 3, 5)[j])
-        k = ((z - delta + NZ) % NZ) // 2
-        for b_ in range(NB):
-            reach = 4 if b_ < 2 else 3
-            block = xb.at[k, b_]
-            sem = x_sem.at[k * NB + b_]
-            arrived(block, sem)
-            if j < 3:
-                remote(block, block, sem, right_z, delta < reach)
-                remote(
-                    block,
-                    block,
-                    sem,
-                    left_z,
-                    jnp.logical_or(
-                        delta == 0, jnp.logical_and(delta > reach, 8 - delta < 7 - reach)
-                    ),
-                )
-            else:
-                remote(block, block, sem, right_z, delta < reach)
-                remote(
-                    block,
-                    block,
-                    sem,
-                    left_z,
-                    jnp.logical_and(delta > reach, 8 - delta < 7 - reach),
-                )
-        return k
-
-    def project(k, start):
-        for b_ in range(NB):
-            raw = xb[k, b_].astype(F32)
-            rows = raw[:NROWS]
-            gain = raw[NROWS : NROWS + 1]
-            scaled = (rows * gain).astype(BF)
-            square = rows * rows
-            square = square[:, :128] + square[:, 128:]
-            c_ = b_ // 2
-            h = b_ % 2
-            parts = [
-                jnp.dot(
-                    scaled, wbuf[q, k, c_, h * 256 : h * 256 + 256], preferred_element_type=F32
-                )
-                for q in (0, 1)
-            ]
-            keyval = jnp.concatenate(
-                [wbuf[q, k, c_, 512 + h * 64 : 576 + h * 64] for q in (0, 1)], axis=0
-            )
-            kv = lax.dot_general(
-                scaled, keyval, (((1,), (1,)), ((), ())), preferred_element_type=F32
-            )
-            if start and b_ == 0:
-                ssq[...] = square
-                qacc[:, :256] = parts[0]
-                qacc[:, 256:] = parts[1]
-                kvacc[...] = kv
-            else:
-                ssq[...] += square
-                qacc[:, :256] += parts[0]
-                qacc[:, 256:] += parts[1]
-                kvacc[...] += kv
+            local(xt.at[s], dst, sem, jnp.logical_and(match, here))
+
+    def by_b(values):
+        return jnp.where(
+            b == 0, values[0], jnp.where(b == 1, values[1], jnp.where(b == 2, values[2], values[3]))
+        )
+
+    nearest = [by_b(v) for v in ((0, 1, 2, 3), (1, 0, 3, 2), (2, 2, 1, 1), (3, 3, 0, 0))]
+    if_match = [(0, i) for i in range(4)]
+    if_match += [(d, i) for i in range(4) for d in (2, 6)]
+    if_match += [(4, i) for i in range(4)]
+    if_not = [(d, i) for i in range(4) for d in (1, 7)]
+    if_not += [(d, i) for i in range(4) for d in (3, 5)]
+    blocks = []
+    for (d_m, i_m), (d_n, i_n) in zip(if_match, if_not):
+        delta = jnp.where(match, d_m, d_n)
+        b_ = jnp.where(match, nearest[i_m], nearest[i_n])
+        blocks.append((delta, ((z - delta + NZ) % NZ) // 2, b_))
+
+    def forward(n):
+        delta, k, b_ = blocks[n]
+        reach = jnp.where(b_ < 2, 4, 3)
+        block = xb.at[k, b_]
+        sem = x_sem.at[k * NB + b_]
+        arrived(block, sem)
+        if n < 4:
+            onward = delta == 0
+        else:
+            onward = False
+        onward = jnp.logical_or(
+            onward, jnp.logical_and(delta > reach, 8 - delta < 7 - reach)
+        )
+        remote(block, block, sem, right_z, delta < reach)
+        remote(block, block, sem, left_z, onward)
+
+    def project(n):
+        _, k, b_ = blocks[n]
+        c_ = b_ // 2
+        h = b_ % 2
+        raw = xb[k, b_].astype(F32)
+        rows = raw[:NROWS]
+        gain = raw[NROWS : NROWS + 1]
+        scaled = (rows * gain).astype(BF)
+        square = rows * rows
+        square = square[:, :128] + square[:, 128:]
+        parts = [
+            jnp.dot(scaled, wbuf[q, k, c_, pl.ds(h * 256, 256)], preferred_element_type=F32)
+            for q in (0, 1)
+        ]
+        keyval = jnp.concatenate(
+            [wbuf[q, k, c_, pl.ds(512 + h * 64, 64)] for q in (0, 1)], axis=0
+        )
+        kv = lax.dot_general(
+            scaled, keyval, (((1,), (1,)), ((), ())), preferred_element_type=F32
+        )
+        if n == 0:
+            ssq[...] = square
+            qacc[:, :256] = parts[0]
+            qacc[:, 256:] = parts[1]
+            kvacc[...] = kv
+        else:
+            ssq[...] += square
+            qacc[:, :256] += parts[0]
+            qacc[:, 256:] += parts[1]
+            kvacc[...] += kv
 
     wqkv.last(bset)
     wqkv.last(1 - bset)
+    for n in range(4):
+        forward(n)
+    wqkv.finish()
     wout.first()
-    ks = [gather_z(0)]
-    ks.append(gather_z(1))
-    wqkv.finish()
-    wout.second()
-    project(ks[0], True)
-    ks.append(gather_z(2))
-    project(ks[1], False)
-    wout.relay(bset)
-    ks.append(gather_z(3))
-    project(ks[2], False)
-    project(ks[3], False)
-
-    for_partner = 1 - zpar
-    remote(xt.at[for_partner], res, res_sem, dev(dpi(x, for_partner, c), tn), match)
-    local(xt.at[yh], res, res_sem, match)
+    for n in range(4):
+        project(n)
+    for n in range(4, 16):
+        forward(n)
+        if n == 6:
+            for i in range(NB):
+                b2 = (b + i) % NB
+                to(cache_ref.at[pl.ds(b2 * 10, 10)], cbuf.at[b], c_sem, dp, z * NB + b2)
+        if n == 8:
+            for_partner = 1 - zpar
+            remote(xt.at[for_partner], res, res_sem, dev(dpi(x, for_partner, c), tn), match)
+            local(xt.at[yh], res, res_sem, match)
+        if n == 10:
+            wout.second()
+        if n == 14:
+            wout.relay(bset)
+        project(n)
 
     diagonal = row40 == lane40
     row8 = lax.broadcasted_iota(jnp.int32, (8, 128), 0)
@@ -510,61 +513,63 @@
         [arecv[i].astype(F32)[:QROWS] for i in range(NB)], axis=0
     ).astype(BF)
 
-    for j in range(4):
-        delta = jnp.where(match, (4, 2, 6, 0)[j], (3, 5, 1, 7)[j])
+    cross = ((2, 0), (3, 1), (0, 2), (1, 3))
+    if_match = [(4, i) for i in range(4)]
+    if_match += [item for i, j in cross for item in ((2, i), (6, j))]
+    if_match += [(0, i) for i in (2, 0, 3, 1)]
+    if_not = [item for i, j in cross for item in ((3, i), (5, j))]
+    if_not += [item for i, j in cross for item in ((1, i), (7, j))]
+    for n in range(16):
+        (d_m, i_m), (d_n, i_n) = if_match[n], if_not[n]
+        delta = jnp.where(match, d_m, d_n)
+        b_ = jnp.where(match, i_m, i_n)
         k = ((z + delta) % NZ) // 2
+        reach = jnp.where(b_ < 2, 4, 3)
         is_end = delta == 0
-        for b_ in range(NB):
-            reach = 4 if b_ < 2 else 3
-            c_ = b_ // 2
-            h = b_ % 2
-            part = jnp.dot(
-                att[:, :256],
-                wobuf[0, k, c_, :, h * 256 : h * 256 + 256],
-                preferred_element_type=F32,
+        c_ = b_ // 2
+        h = b_ % 2
+        part = jnp.dot(
+            att[:, :256], wobuf[0, k, c_, :, pl.ds(h * 256, 256)], preferred_element_type=F32
+        )
+        acc[...] = part + jnp.dot(
+            att[:, 256:], wobuf[1, k, c_, :, pl.ds(h * 256, 256)], preferred_element_type=F32
+        )
+        from_left = delta + 1 <= reach
+        from_right = jnp.logical_or(delta > reach + 1, is_end)
+        index = k * NB + b_
+
+        @pl.when(from_left)
+        def _(index=index, k=k, b_=b_):
+            arrived(rright.at[k, b_], rr_sem.at[index])
+            acc[...] += rright[k, b_].astype(F32)
+
+        @pl.when(from_right)
+        def _(index=index, k=k, b_=b_):
+            arrived(rleft.at[k, b_], rl_sem.at[index])
+            acc[...] += rleft[k, b_].astype(F32)
+
+        src = sbuf.at[k, b_]
+        src[...] = acc[...].astype(BF)
+        remote(
+            src,
+            rright.at[k, b_],
+            rr_sem.at[index],
+            right_z,
+            jnp.logical_and(delta >= 1, delta <= reach),
+        )
+        remote(src, rleft.at[k, b_], rl_sem.at[index], left_z, delta > reach)
+        if n >= 12:
+            dp_ = dpi(x, bset, c)
+            tn_ = z * NB + b_
+            here = jnp.logical_and(dp_ == dp, tn_ == tn)
+            remote(
+                src,
+                frecv.at[pair],
+                f_sem.at[pair],
+                dev(dp_, tn_),
+                jnp.logical_and(is_end, jnp.logical_not(here)),
             )
-            part = part + jnp.dot(
-                att[:, 256:],
-                wobuf[1, k, c_, :, h * 256 : h * 256 + 256],
-                preferred_element_type=F32,
-            )
-            acc[...] = part
-            go_right = jnp.logical_and(delta >= 1, delta <= reach)
-            go_left = delta > reach
-            from_left = delta + 1 <= reach
-            from_right = jnp.logical_or(delta > reach + 1, is_end)
-            index = k * NB + b_
-
-            @pl.when(from_left)
-            def _(index=index, k=k, b_=b_):
-                arrived(rright.at[k, b_], rr_sem.at[index])
-                acc[...] += rright[k, b_].astype(F32)
-
-            @pl.when(from_right)
-            def _(index=index, k=k, b_=b_):
-                arrived(rleft.at[k, b_], rl_sem.at[index])
-                acc[...] += rleft[k, b_].astype(F32)
-
-            sbuf[k, b_] = acc[...].astype(BF)
-            remote(sbuf.at[k, b_], rright.at[k, b_], rr_sem.at[index], right_z, go_right)
-            remote(sbuf.at[k, b_], rleft.at[k, b_], rl_sem.at[index], left_z, go_left)
-            if j == 3:
-                dp_ = dpi(x, bset, c)
-                tn_ = z * NB + b_
-                here = jnp.logical_and(dp_ == dp, tn_ == tn)
-                remote(
-                    sbuf.at[k, b_],
-                    frecv.at[pair],
-                    f_sem.at[pair],
-                    dev(dp_, tn_),
-                    jnp.logical_and(is_end, jnp.logical_not(here)),
-                )
-                local(
-                    sbuf.at[k, b_],
-                    frecv.at[pair],
-                    f_sem.at[pair],
-                    jnp.logical_and(is_end, here),
-                )
+            local(src, frecv.at[pair], f_sem.at[pair], jnp.logical_and(is_end, here))
 
     arrived(res, res_sem)
     for p in (0, 1):
@@ -593,8 +598,6 @@
 def body(
     token_ids, lengths, embed_table, norm_gain, w_query, key_value_weight, w_out, key_value_cache
 ):
-    numbers = jnp.concatenate([token_ids, lengths[None]], axis=0)
-    numbers = jnp.pad(numbers, ((0, 3), (0, 88)))
     table = embed_table.reshape(16, -1)
     gain = norm_gain.reshape(1, -1)
     frequency = THETA ** (-(np.arange(64) / 64))
@@ -608,12 +611,12 @@
     out = pl.pallas_call(
         kernel,
         out_shape=jax.ShapeDtypeStruct((NROWS, 256), BF),
-        in_specs=[vmem, anywhere, vmem, vmem, anywhere, anywhere, anywhere, anywhere],
+        in_specs=[vmem, vmem, anywhere, vmem, vmem, anywhere, anywhere, anywhere, anywhere],
         out_specs=vmem,
         scratch_shapes=[
             pltpu.VMEM((16, 81920), BF),
-            pltpu.VMEM((16, 8, 128), jnp.int32),
-            pltpu.SMEM((16, 8, 128), jnp.int32),
+            pltpu.VMEM((16, 4, 40), jnp.int32),
+            pltpu.SMEM((16, 4, 40), jnp.int32),
             pltpu.VMEM((8, 2, 16, 256), BF),
             pltpu.VMEM((QROWS, HEAD), F32),
             pltpu.VMEM((QROWS, HEAD), F32),
@@ -656,7 +659,7 @@
             collective_id=0, has_side_effects=True, vmem_limit_bytes=56 * 1024 * 1024
         ),
         name="decode_block",
-    )(numbers, table, gain, frequency, w_query, keyval, w_out, cache)
+    )(token_ids, lengths[None], table, gain, frequency, w_query, keyval, w_out, cache)
     return out.reshape(4, 40, 256)
 
 

time: 131 us -> 116 us (0.89)
  the two profiles are of different devices: /device:TPU:56 before, /device:TPU:72 now
where the time goes in v3:
time: 116 us; the launch traced here: 115 us
  Pallas kernels  113 us (97%)
  local copies, waits for them, and re-layouts  2.75 us (2%)
    pallas_call x1, Pallas kernels, body(): pl.pallas_call(kernel, out_shape=jax.ShapeDtypeStruct((NROWS, 256), BF),...  113 us

profile of v3, /device:TPU:72, one launch (start us, length us, event | category | flops | bytes accessed | tf_op | source)
XLA Modules:
  0.0 115.4 jit_solution(4703092809367765112)
XLA Ops:
  0.0 1.2 %reshape.13.gain_ref = bf16[1,256]{1,0:T(2,128)(2,1)} reshape(bf16[256]{0:T(256)(128)(2,1)} %param.12) | data formatting | bytes 1024 | tf_op jit(solution)/shard_map/reshape | solution.py:602
  1.2 112.6 %decode_block.1 = bf16[160,256]{1,0:T(8,128)(2,1)} custom-call(s32[4,40]{1,0:T(4,128)} %tok_ref.1, s32[1,40]{1,0:T(1,128)} %bitcast.9, bf16[16,81920]{1,0:T(8,128)(2,1)} %bitcast.5, bf16[1,256]{1,0:T(2,128)(2,1)} %reshape.13.gain_ref, f32[1,128]{1,0:T(1,128)} %constant.2.clone.freq_ref, bf16[512,256]{1,0:T(8,128)(2,1)} %wq_ref.1, bf16[64,512]{1,0:T(8,128)(2,1)} %bitcast.8, ...), custom_call_target="tpu_custom_call" | custom-call | tf_op jit(solution)/shard_map/decode_block/pallas_call | solution.py:611
  113.9 1.5 %copy.11 = bf16[4,40,256]{2,1,0:T(8,128)(2,1)} copy(bf16[4,40,256]{2,1,0:T(8,128)(2,1)} %bitcast.7) | data formatting | bytes 163840

commit v4 on v3

--- a/solution.py
+++ b/solution.py
@@ -167,16 +167,6 @@
         pl.semaphore_signal(barrier, inc=1, device_id=where, device_id_type=MESH)
         partners += 1
 
-    row40 = lax.broadcasted_iota(jnp.int32, (QROWS, 128), 0)
-    lane40 = lax.broadcasted_iota(jnp.int32, (QROWS, 128), 1)
-    lengths = len_ref[...].astype(F32)
-    row_of = lax.broadcasted_iota(jnp.int32, (QROWS, 40), 0) // 4 + b * 10
-    all_rows = lax.broadcasted_iota(jnp.int32, (QROWS, 40), 1)
-    length = jnp.sum(jnp.where(all_rows == row_of, lengths, 0.0), axis=1, keepdims=True)
-    turn = (length + (row40 % 4).astype(F32)) * freq_ref[...]
-    cos_ref[...] = jnp.cos(turn)
-    sin_ref[...] = jnp.where(lane40 < HEAD // 2, -1.0, 1.0) * jnp.sin(turn)
-
     pl.semaphore_wait(barrier, partners)
 
     for i in range(1, 16):
@@ -252,7 +242,7 @@
     wide = lax.broadcasted_iota(jnp.int32, (16, 256), 1)
     feature = lax.broadcasted_iota(jnp.int32, (16, 256), 0)
     gain_column = jnp.sum(
-        jnp.where(wide == dp * 16 + feature, gain_ref[...].astype(F32), 0.0),
+        jnp.where(wide == dp * 16 + feature, gain_ref[...].astype(F32)[None], 0.0),
         axis=1,
         keepdims=True,
     )
@@ -299,7 +289,6 @@
     wqkv.second()
     wqkv.relay(bset)
     lax.fori_loop(4, 8, lookup, 0)
-    wqkv.relay(1 - bset)
 
     k_here = z // 2
 
@@ -341,6 +330,19 @@
         delta = jnp.where(match, d_m, d_n)
         b_ = jnp.where(match, nearest[i_m], nearest[i_n])
         blocks.append((delta, ((z - delta + NZ) % NZ) // 2, b_))
+
+    row40 = lax.broadcasted_iota(jnp.int32, (QROWS, 128), 0)
+    lane40 = lax.broadcasted_iota(jnp.int32, (QROWS, 128), 1)
+
+    def angles():
+        lengths = len_ref[...].astype(F32)
+        row_of = lax.broadcasted_iota(jnp.int32, (QROWS, 40), 0) // 4 + b * 10
+        all_rows = lax.broadcasted_iota(jnp.int32, (QROWS, 40), 1)
+        length = jnp.sum(jnp.where(all_rows == row_of, lengths, 0.0), axis=1, keepdims=True)
+        turn = (length + (row40 % 4).astype(F32)) * freq_ref[...]
+        cos_ref[...] = jnp.cos(turn)
+        sin_ref[...] = jnp.where(lane40 < HEAD // 2, -1.0, 1.0) * jnp.sin(turn)
+        return length
 
     def forward(n):
         delta, k, b_ = blocks[n]
@@ -389,16 +391,18 @@
             qacc[:, 256:] += parts[1]
             kvacc[...] += kv
 
+    forward(0)
+    wqkv.relay(1 - bset)
+    forward(1)
     wqkv.last(bset)
+    forward(2)
+    forward(3)
     wqkv.last(1 - bset)
-    for n in range(4):
-        forward(n)
-    wqkv.finish()
-    wout.first()
-    for n in range(4):
-        project(n)
     for n in range(4, 16):
         forward(n)
+        if n == 4:
+            wout.first()
+            length = angles()
         if n == 6:
             for i in range(NB):
                 b2 = (b + i) % NB
@@ -407,11 +411,16 @@
             for_partner = 1 - zpar
             remote(xt.at[for_partner], res, res_sem, dev(dpi(x, for_partner, c), tn), match)
             local(xt.at[yh], res, res_sem, match)
-        if n == 10:
+        if n == 9:
             wout.second()
         if n == 14:
             wout.relay(bset)
-        project(n)
+        if n == 7:
+            wqkv.finish()
+        if n >= 7:
+            for m in range(2 * (n - 7), min(2 * (n - 7) + 2, n + 1)):
+                project(m)
+    project(15)
 
     diagonal = row40 == lane40
     row8 = lax.broadcasted_iota(jnp.int32, (8, 128), 0)
@@ -599,7 +608,6 @@
     token_ids, lengths, embed_table, norm_gain, w_query, key_value_weight, w_out, key_value_cache
 ):
     table = embed_table.reshape(16, -1)
-    gain = norm_gain.reshape(1, -1)
     frequency = THETA ** (-(np.arange(64) / 64))
     frequency = jnp.asarray(np.concatenate([frequency, frequency])[None], F32)
     keyval = key_value_weight.T
@@ -659,7 +667,7 @@
             collective_id=0, has_side_effects=True, vmem_limit_bytes=56 * 1024 * 1024
         ),
         name="decode_block",
-    )(token_ids, lengths[None], table, gain, frequency, w_query, keyval, w_out, cache)
+    )(token_ids, lengths[None], table, norm_gain, frequency, w_query, keyval, w_out, cache)
     return out.reshape(4, 40, 256)
 
 

time: 116 us -> 116 us (level)
  the two profiles are of different devices: /device:TPU:72 before, /device:TPU:42 now
where the time goes in v4:
time: 116 us
  Pallas kernels  115 us (99%)
  local copies, waits for them, and re-layouts  1.53 us (1%)
    pallas_call x1, Pallas kernels, body(): pl.pallas_call(kernel, out_shape=jax.ShapeDtypeStruct((NROWS, 256), BF),...  115 us

profile of v4, /device:TPU:42, one launch (start us, length us, event | category | flops | bytes accessed | tf_op | source)
XLA Modules:
  0.0 116.2 jit_solution(9290949353043940806)
XLA Ops:
  0.0 114.6 %decode_block.1 = bf16[160,256]{1,0:T(8,128)(2,1)} custom-call(s32[4,40]{1,0:T(4,128)} %tok_ref.1, s32[1,40]{1,0:T(1,128)} %bitcast.9, bf16[16,81920]{1,0:T(8,128)(2,1)} %bitcast.5, bf16[256]{0:T(256)(128)(2,1)} %gain_ref.1, f32[1,128]{1,0:T(1,128)} %constant.2.clone.freq_ref, bf16[512,256]{1,0:T(8,128)(2,1)} %wq_ref.1, bf16[64,512]{1,0:T(8,128)(2,1)} %bitcast.8, ...), custom_call_target="tpu_custom_call" | custom-call | tf_op jit(solution)/shard_map/decode_block/pallas_call | solution.py:619
  114.6 1.5 %copy.11 = bf16[4,40,256]{2,1,0:T(8,128)(2,1)} copy(bf16[4,40,256]{2,1,0:T(8,128)(2,1)} %bitcast.7) | data formatting | bytes 163840

commit v5 on v4

--- a/solution.py
+++ b/solution.py
@@ -47,7 +47,6 @@
     lrecv,
     xt,
     xb,
-    res,
     wbuf,
     wobuf,
     cbuf,
@@ -69,7 +68,6 @@
     tok_sem,
     l_sem,
     x_sem,
-    res_sem,
     w_sem,
     wo_sem,
     c_sem,
@@ -142,6 +140,7 @@
 
     table_copy = pltpu.make_async_copy(table_ref, tab, loc_sem.at[0])
     table_copy.start()
+    local(tok_ref, tokv.at[dp], tok_sem.at[dp])
     own_shard = wbuf.at[bset, x, c]
     own_sem = w_sem.at[((bset * NX + x) * 2 + c) * 2]
     local(wq_ref, own_shard.at[pl.ds(0, 512)], own_sem)
@@ -170,8 +169,7 @@
     pl.semaphore_wait(barrier, partners)
 
     for i in range(1, 16):
-        remote(tok_ref, tokv.at[dp], tok_sem, dev((dp + i) % 16, tn))
-    local(tok_ref, tokv.at[dp], tok_sem)
+        remote(tok_ref, tokv.at[dp], tok_sem.at[dp], dev((dp + i) % 16, tn))
 
     class Gather:
         def __init__(self, buf, sem, half):
@@ -189,11 +187,15 @@
         def send(self, src, q, x_, where):
             remote(src, self.slot(q, x_, c), self.s(q, x_, c), where)
 
-        def first(self):
+        def to_pair(self):
             own = (bset, x)
             src = self.slot(*own, c)
             arrived(src, self.s(*own, c))
             self.send(src, *own, dev(dp, z * NB + pair * 2 + 1 - bset))
+
+        def first(self):
+            own = (bset, x)
+            src = self.slot(*own, c)
             self.send(src, *own, dev(dpi(xr, yh, c), tn))
             self.send(src, *own, dev(dpi(xl, yh, c), tn))
             self.send(src, *own, dev(dpi(x, yh, 1 - c), tn))
@@ -229,13 +231,27 @@
 
     wqkv = Gather(wbuf, w_sem, 320)
     wout = Gather(wobuf, wo_sem, 128)
+    wqkv.to_pair()
     wqkv.first()
     local(wo_ref, wout.slot(bset, x, c), wout.s(bset, x, c))
 
-    arrived(tokv, tok_sem)
-    to_scalar = pltpu.make_async_copy(tokv, toks, loc_sem.at[1])
-    to_scalar.start()
-    to_scalar.wait()
+    place = x * 2 + c
+
+    def source(i):
+        e = (place + i % 8) % 8
+        s = (yh + i // 8) % 2
+        return e, s, dpi(e // 2, s, e % 2)
+
+    def to_scalar(i):
+        _, _, d2 = source(i)
+        return pltpu.make_async_copy(tokv.at[d2], toks.at[d2], loc_sem.at[1 + i % 2])
+
+    def fetch(i):
+        _, _, d2 = source(i)
+        arrived(tokv.at[d2], tok_sem.at[d2])
+        to_scalar(i).start()
+
+    fetch(0)
     table_copy.wait()
 
     lane = lax.broadcasted_iota(jnp.int32, (16, 128), 1)
@@ -247,7 +263,6 @@
         keepdims=True,
     )
     gain_tail = jnp.where(lane == NROWS - 128, gain_column, 0.0)
-    place = x * 2 + c
     lookup_base = counter[0]
     counter[0] += 8
 
@@ -263,32 +278,31 @@
         )
 
     def lookup(i, carry):
-        e = (place + 1 + i) % 8
-
-        def one_set(s, carry):
-            d2 = dpi(e // 2, s, e % 2)
-            for half, count in ((0, 128), (1, NROWS - 128)):
-                found = jnp.zeros((16, 128), F32) if half == 0 else gain_tail
-                for n in range(count):
-                    row = half * 128 + n
-                    token = toks[d2, row % 4, row // 4]
-                    block = lax.shift_right_logical(token, 7)
-                    tile = tab[:, pl.ds(block * 128, 128)].astype(F32)
-                    picked = jnp.where(lane == jnp.bitwise_and(token, 127), tile, 0.0)
-                    found = jnp.where(lane == n, jnp.sum(picked, axis=1, keepdims=True), found)
-                lsend[e, s, :, pl.ds(half * 128, 128)] = found.astype(BF)
-            return carry
-
-        lax.fori_loop(0, 2, one_set, 0)
-        dp2, copy = lookup_copy(e)
-        pl.when(dp2 != dp)(copy.start)
-        pl.when(dp2 == dp)(pltpu.make_async_copy(lsend.at[e], lrecv.at[dp], l_sem).start)
+        e, s, d2 = source(i)
+        pl.when(i < 15)(lambda: fetch(i + 1))
+        to_scalar(i).wait()
+        for half, count in ((0, 128), (1, NROWS - 128)):
+            found = jnp.zeros((16, 128), F32) if half == 0 else gain_tail
+            for n in range(count):
+                row = half * 128 + n
+                token = toks[d2, row % 4, row // 4]
+                block = lax.shift_right_logical(token, 7)
+                tile = tab[:, pl.ds(block * 128, 128)].astype(F32)
+                picked = jnp.where(lane == jnp.bitwise_and(token, 127), tile, 0.0)
+                found = jnp.where(lane == n, jnp.sum(picked, axis=1, keepdims=True), found)
+            lsend[e, s, :, pl.ds(half * 128, 128)] = found.astype(BF)
+
+        @pl.when(i >= 8)
+        def _():
+            dp2, copy = lookup_copy(e)
+            pl.when(dp2 != dp)(copy.start)
+            pl.when(dp2 == dp)(pltpu.make_async_copy(lsend.at[e], lrecv.at[dp], l_sem).start)
+
         return carry
 
-    lax.fori_loop(0, 4, lookup, 0)
+    lax.fori_loop(0, 16, lookup, 0)
     wqkv.second()
     wqkv.relay(bset)
-    lax.fori_loop(4, 8, lookup, 0)
 
     k_here = z // 2
 
@@ -397,30 +411,26 @@
     wqkv.last(bset)
     forward(2)
     forward(3)
+    wout.to_pair()
     wqkv.last(1 - bset)
     for n in range(4, 16):
         forward(n)
-        if n == 4:
+        if n == 5:
             wout.first()
-            length = angles()
-        if n == 6:
+        if n == 8:
             for i in range(NB):
                 b2 = (b + i) % NB
                 to(cache_ref.at[pl.ds(b2 * 10, 10)], cbuf.at[b], c_sem, dp, z * NB + b2)
-        if n == 8:
-            for_partner = 1 - zpar
-            remote(xt.at[for_partner], res, res_sem, dev(dpi(x, for_partner, c), tn), match)
-            local(xt.at[yh], res, res_sem, match)
         if n == 9:
             wout.second()
+        if n == 11:
+            wqkv.finish()
+            for m in range(11):
+                project(m)
+        if n >= 11:
+            project(n)
         if n == 14:
             wout.relay(bset)
-        if n == 7:
-            wqkv.finish()
-        if n >= 7:
-            for m in range(2 * (n - 7), min(2 * (n - 7) + 2, n + 1)):
-                project(m)
-    project(15)
 
     diagonal = row40 == lane40
     row8 = lax.broadcasted_iota(jnp.int32, (8, 128), 0)
@@ -445,6 +455,19 @@
 
     wout.relay(1 - bset)
 
+    length = angles()
+    col = lax.broadcasted_iota(jnp.int32, (QROWS, 640), 1)
+    row = lax.broadcasted_iota(jnp.int32, (QROWS, 640), 0) // 4
+    within = col % 160
+    position = (col // 160) * 16 + within % 16
+    old_ok = jnp.logical_and(within // 16 == row, position.astype(F32) < length)
+    new_ok = jnp.logical_and(
+        lane40 // 4 == row40 // 4, jnp.logical_and(lane40 <= row40, lane40 < QROWS)
+    )
+    old_bias = jnp.where(old_ok, 0.0, -1e30)
+    new_bias = jnp.where(new_ok, 0.0, -1e30)
+    old_bias = jnp.concatenate([old_bias] * 8, axis=0)
+    new_bias = jnp.concatenate([new_bias] * 8, axis=0)
     for i in range(NB):
         arrived(qrecv.at[i // 2, i % 2], q_sem.at[i])
     arrived(cbuf, c_sem)
@@ -481,18 +504,6 @@
     scores_new = (
         lax.dot_general(query, key_new, contract_last, preferred_element_type=F32) * inv_root
     )
-    col = lax.broadcasted_iota(jnp.int32, (QROWS, 640), 1)
-    row = lax.broadcasted_iota(jnp.int32, (QROWS, 640), 0) // 4
-    within = col % 160
-    position = (col // 160) * 16 + within % 16
-    old_ok = jnp.logical_and(within // 16 == row, position.astype(F32) < length)
-    new_ok = jnp.logical_and(
-        lane40 // 4 == row40 // 4, jnp.logical_and(lane40 <= row40, lane40 < QROWS)
-    )
-    old_bias = jnp.where(old_ok, 0.0, -1e30)
-    new_bias = jnp.where(new_ok, 0.0, -1e30)
-    old_bias = jnp.concatenate([old_bias] * 8, axis=0)
-    new_bias = jnp.concatenate([new_bias] * 8, axis=0)
     scores_old = jnp.where(old_bias == 0.0, scores_old, -1e30)
     scores_new = jnp.where(new_bias == 0.0, scores_new, -1e30)
     top = jnp.maximum(
@@ -557,6 +568,12 @@
             arrived(rleft.at[k, b_], rl_sem.at[index])
             acc[...] += rleft[k, b_].astype(F32)
 
+        if n >= 12:
+
+            @pl.when(jnp.logical_and(is_end, pair == 0))
+            def _(k=k, b_=b_):
+                acc[...] += xb[k, b_, :NROWS].astype(F32)
+
         src = sbuf.at[k, b_]
         src[...] = acc[...].astype(BF)
         remote(
@@ -580,10 +597,9 @@
             )
             local(src, frecv.at[pair], f_sem.at[pair], jnp.logical_and(is_end, here))
 
-    arrived(res, res_sem)
     for p in (0, 1):
         arrived(frecv.at[p], f_sem.at[p])
-    hidden = res[:NROWS].astype(F32) + (frecv[0].astype(F32) + frecv[1].astype(F32))
+    hidden = frecv[0].astype(F32) + frecv[1].astype(F32)
     hidden = jnp.concatenate([hidden, jnp.zeros((256 - NROWS, 256), F32)], axis=0).astype(BF)
     to_row = lax.broadcasted_iota(jnp.int32, (NROWS, 256), 0)
     from_row = lax.broadcasted_iota(jnp.int32, (NROWS, 256), 1)
@@ -631,7 +647,6 @@
             pltpu.VMEM((16, 2, 16, 256), BF),
             pltpu.VMEM((2, XROWS, 256), BF),
             pltpu.VMEM((4, NB, XROWS, 256), BF),
-            pltpu.VMEM((XROWS, 256), BF),
             pltpu.VMEM((2, NX, 2, 640, 256), BF),
             pltpu.VMEM((2, NX, 2, 256, 512), BF),
             pltpu.VMEM((NB, 10, 16, 256), BF),
@@ -649,11 +664,10 @@
             pltpu.VMEM((4, NB, NROWS, 256), BF),
             pltpu.VMEM((2, NROWS, 256), BF),
             dma((192,)),
-            dma((2,)),
-            dma,
+            dma((3,)),
+            dma((16,)),
             dma,
             dma((16,)),
-            dma,
             dma((32,)),
             dma((32,)),
             dma,

time: 116 us -> 105 us (0.905)
  the two profiles are of different devices: /device:TPU:42 before, /device:TPU:72 now
where the time goes in v5:
time: 105 us
  Pallas kernels  104 us (99%)
  local copies, waits for them, and re-layouts  1.53 us (1%)
    pallas_call x1, Pallas kernels, body(): pl.pallas_call(kernel, out_shape=jax.ShapeDtypeStruct((NROWS, 256), BF),...  104 us

profile of v5, /device:TPU:72, one launch (start us, length us, event | category | flops | bytes accessed | tf_op | source)
XLA Modules:
  0.0 105.0 jit_solution(15384201371407973624)
XLA Ops:
  0.0 103.5 %decode_block.1 = bf16[160,256]{1,0:T(8,128)(2,1)} custom-call(s32[4,40]{1,0:T(4,128)} %tok_ref.1, s32[1,40]{1,0:T(1,128)} %bitcast.9, bf16[16,81920]{1,0:T(8,128)(2,1)} %bitcast.5, bf16[256]{0:T(256)(128)(2,1)} %gain_ref.1, f32[1,128]{1,0:T(1,128)} %constant.2.clone.freq_ref, bf16[512,256]{1,0:T(8,128)(2,1)} %wq_ref.1, bf16[64,512]{1,0:T(8,128)(2,1)} %bitcast.8, ...), custom_call_target="tpu_custom_call" | custom-call | tf_op jit(solution)/shard_map/decode_block/pallas_call | solution.py:635
  103.5 1.5 %copy.11 = bf16[4,40,256]{2,1,0:T(8,128)(2,1)} copy(bf16[4,40,256]{2,1,0:T(8,128)(2,1)} %bitcast.7) | data formatting | bytes 163840

commit v6 on v5

--- a/solution.py
+++ b/solution.py
@@ -96,9 +96,10 @@
         return (x_ * 2 + yh_) * 2 + c_
 
     pending = []
+    pending_out = []
     counter = [0]
 
-    def remote(src, dst, rsem, where, cond=None):
+    def remote(src, dst, rsem, where, cond=None, sink=pending):
         n = counter[0]
         counter[0] += 1
         copy = pltpu.make_async_remote_copy(
@@ -113,7 +114,16 @@
             copy.start()
         else:
             pl.when(cond)(copy.start)
-        pending.append((cond, copy))
+        sink.append((cond, copy))
+
+    def sent(sink, count=None):
+        done = sink[:count]
+        del sink[:count]
+        for cond, copy in done:
+            if cond is None:
+                copy.wait_send()
+            else:
+                pl.when(cond)(copy.wait_send)
 
     def local(src, dst, sem, cond=None):
         copy = pltpu.make_async_copy(src, dst, sem)
@@ -169,11 +179,13 @@
     pl.semaphore_wait(barrier, partners)
 
     for i in range(1, 16):
-        remote(tok_ref, tokv.at[dp], tok_sem.at[dp], dev((dp + i) % 16, tn))
+        e_ = (x * 2 + c + 8 - i % 8) % 8
+        there = dpi(e_ // 2, (yh + i // 8) % 2, e_ % 2)
+        remote(tok_ref, tokv.at[dp], tok_sem.at[dp], dev(there, tn))
 
     class Gather:
-        def __init__(self, buf, sem, half):
-            self.buf, self.sem, self.half = buf, sem, half
+        def __init__(self, buf, sem, half, sink):
+            self.buf, self.sem, self.half, self.sink = buf, sem, half, sink
 
         def slot(self, q, x_, c_, h=None):
             ref = self.buf.at[q, x_, c_]
@@ -185,7 +197,7 @@
             return self.sem.at[((q * NX + x_) * 2 + c_) * 2 + h]
 
         def send(self, src, q, x_, where):
-            remote(src, self.slot(q, x_, c), self.s(q, x_, c), where)
+            remote(src, self.slot(q, x_, c), self.s(q, x_, c), where, sink=self.sink)
 
         def to_pair(self):
             own = (bset, x)
@@ -216,6 +228,7 @@
                     self.slot(q, x_, c, h),
                     self.s(q, x_, c, h),
                     dev(dpi(to_x, yh, c), tn),
+                    sink=self.sink,
                 )
                 self.send(self.slot(q, x_, c), q, x_, dev(dpi(x, yh, 1 - c), tn))
 
@@ -229,8 +242,8 @@
                 for x_ in range(NX):
                     arrived(self.slot(q, x_, 1 - c), self.s(q, x_, 1 - c))
 
-    wqkv = Gather(wbuf, w_sem, 320)
-    wout = Gather(wobuf, wo_sem, 128)
+    wqkv = Gather(wbuf, w_sem, 320, pending)
+    wout = Gather(wobuf, wo_sem, 128, pending_out)
     wqkv.to_pair()
     wqkv.first()
     local(wo_ref, wout.slot(bset, x, c), wout.s(bset, x, c))
@@ -315,7 +328,7 @@
             xt[s] = features.T[:XROWS].astype(BF)
 
         for h in (0, 1):
-            b2 = s + 2 * h
+            b2 = (1 - pair if h == 0 else pair) * 2 + s
             here = b2 == b
             dst = xb.at[k_here, b]
             sem = x_sem.at[k_here * NB + b]
@@ -432,6 +445,8 @@
         if n == 14:
             wout.relay(bset)
 
+    before_q = len(pending)
+
     diagonal = row40 == lane40
     row8 = lax.broadcasted_iota(jnp.int32, (8, 128), 0)
     for i in range(NB):
@@ -468,6 +483,15 @@
     new_bias = jnp.where(new_ok, 0.0, -1e30)
     old_bias = jnp.concatenate([old_bias] * 8, axis=0)
     new_bias = jnp.concatenate([new_bias] * 8, axis=0)
+    sent(pending, before_q)
+
+    def lookup_sent(e, carry):
+        dp2, copy = lookup_copy(e)
+        pl.when(dp2 != dp)(copy.wait_send)
+        return carry
+
+    lax.fori_loop(0, 8, lookup_sent, 0)
+
     for i in range(NB):
         arrived(qrecv.at[i // 2, i % 2], q_sem.at[i])
     arrived(cbuf, c_sem)
@@ -512,8 +536,9 @@
     exp_old = jnp.exp(scores_old - top)
     exp_new = jnp.exp(scores_new - top)
     totals = jnp.sum(exp_old, axis=1, keepdims=True) + jnp.sum(exp_new, axis=1, keepdims=True)
-    probs_old = (exp_old / totals).astype(BF)
-    probs_new = (exp_new / totals).astype(BF)
+    share = 1.0 / totals
+    probs_old = (exp_old * share).astype(BF)
+    probs_new = (exp_new * share).astype(BF)
     attended = jnp.dot(probs_old, values, preferred_element_type=F32)
     attended = attended + jnp.dot(probs_new, value_new, preferred_element_type=F32)
     for p in (0, 1):
@@ -527,6 +552,7 @@
     wout.last(bset)
     wout.last(1 - bset)
     wout.finish()
+    sent(pending_out)
     for i in range(NB):
         arrived(arecv.at[i], a_sem.at[i])
     att[...] = jnp.concatenate(
@@ -568,6 +594,8 @@
             arrived(rleft.at[k, b_], rl_sem.at[index])
             acc[...] += rleft[k, b_].astype(F32)
 
+        if n == 12:
+            before_end = len(pending)
         if n >= 12:
 
             @pl.when(jnp.logical_and(is_end, pair == 0))
@@ -597,6 +625,7 @@
             )
             local(src, frecv.at[pair], f_sem.at[pair], jnp.logical_and(is_end, here))
 
+    sent(pending, before_end)
     for p in (0, 1):
         arrived(frecv.at[p], f_sem.at[p])
     hidden = frecv[0].astype(F32) + frecv[1].astype(F32)
@@ -606,18 +635,7 @@
     order = jnp.where(from_row == (to_row % 40) * 4 + to_row // 40, 1.0, 0.0).astype(BF)
     out_ref[...] = jnp.dot(order, hidden, preferred_element_type=F32).astype(BF)
 
-    for cond, copy in pending:
-        if cond is None:
-            copy.wait_send()
-        else:
-            pl.when(cond)(copy.wait_send)
-
-    def lookup_sent(e, carry):
-        dp2, copy = lookup_copy(e)
-        pl.when(dp2 != dp)(copy.wait_send)
-        return carry
-
-    lax.fori_loop(0, 8, lookup_sent, 0)
+    sent(pending)
 
 
 def body(

time: 105 us -> 105 us (level)
  no operation moved by 1% of the time
where the time goes in v6:
time: 105 us
  Pallas kernels  103 us (98%)
  local copies, waits for them, and re-layouts  1.53 us (1%)
    pallas_call x1, Pallas kernels, body(): pl.pallas_call(kernel, out_shape=jax.ShapeDtypeStruct((NROWS, 256), BF),...  103 us

profile of v6, /device:TPU:72, one launch (start us, length us, event | category | flops | bytes accessed | tf_op | source)
XLA Modules:
  0.0 104.5 jit_solution(12216002486275929008)
XLA Ops:
  0.0 103.0 %decode_block.1 = bf16[160,256]{1,0:T(8,128)(2,1)} custom-call(s32[4,40]{1,0:T(4,128)} %tok_ref.1, s32[1,40]{1,0:T(1,128)} %bitcast.9, bf16[16,81920]{1,0:T(8,128)(2,1)} %bitcast.5, bf16[256]{0:T(256)(128)(2,1)} %gain_ref.1, f32[1,128]{1,0:T(1,128)} %constant.2.clone.freq_ref, bf16[512,256]{1,0:T(8,128)(2,1)} %wq_ref.1, bf16[64,512]{1,0:T(8,128)(2,1)} %bitcast.8, ...), custom_call_target="tpu_custom_call" | custom-call | tf_op jit(solution)/shard_map/decode_block/pallas_call | solution.py:653
  103.0 1.5 %copy.11 = bf16[4,40,256]{2,1,0:T(8,128)(2,1)} copy(bf16[4,40,256]{2,1,0:T(8,128)(2,1)} %bitcast.7) | data formatting | bytes 163840

commit v7 on v6

--- a/solution.py
+++ b/solution.py
@@ -277,14 +277,14 @@
     )
     gain_tail = jnp.where(lane == NROWS - 128, gain_column, 0.0)
     lookup_base = counter[0]
-    counter[0] += 8
-
-    def lookup_copy(e):
+    counter[0] += 16
+
+    def lookup_copy(e, s):
         dp2 = dpi(e // 2, zpar, e % 2)
         return dp2, pltpu.make_async_remote_copy(
-            src_ref=lsend.at[e],
-            dst_ref=lrecv.at[dp],
-            send_sem=send_sem.at[lookup_base + e],
+            src_ref=lsend.at[e, s],
+            dst_ref=lrecv.at[dp, s],
+            send_sem=send_sem.at[lookup_base + e * 2 + s],
             recv_sem=l_sem,
             device_id=dev(dp2, tn),
             device_id_type=MESH,
@@ -305,12 +305,9 @@
                 found = jnp.where(lane == n, jnp.sum(picked, axis=1, keepdims=True), found)
             lsend[e, s, :, pl.ds(half * 128, 128)] = found.astype(BF)
 
-        @pl.when(i >= 8)
-        def _():
-            dp2, copy = lookup_copy(e)
-            pl.when(dp2 != dp)(copy.start)
-            pl.when(dp2 == dp)(pltpu.make_async_copy(lsend.at[e], lrecv.at[dp], l_sem).start)
-
+        dp2, copy = lookup_copy(e, s)
+        pl.when(dp2 != dp)(copy.start)
+        pl.when(dp2 == dp)(pltpu.make_async_copy(lsend.at[e, s], lrecv.at[dp, s], l_sem).start)
         return carry
 
     lax.fori_loop(0, 16, lookup, 0)
@@ -485,12 +482,12 @@
     new_bias = jnp.concatenate([new_bias] * 8, axis=0)
     sent(pending, before_q)
 
-    def lookup_sent(e, carry):
-        dp2, copy = lookup_copy(e)
+    def lookup_sent(i, carry):
+        dp2, copy = lookup_copy(i // 2, i % 2)
         pl.when(dp2 != dp)(copy.wait_send)
         return carry
 
-    lax.fori_loop(0, 8, lookup_sent, 0)
+    lax.fori_loop(0, 16, lookup_sent, 0)
 
     for i in range(NB):
         arrived(qrecv.at[i // 2, i % 2], q_sem.at[i])

time: 105 us -> 104 us (level)
  no operation moved by 1% of the time
where the time goes in v7:
time: 104 us
  Pallas kernels  103 us (99%)
  local copies, waits for them, and re-layouts  1.53 us (1%)
    pallas_call x1, Pallas kernels, body(): pl.pallas_call(kernel, out_shape=jax.ShapeDtypeStruct((NROWS, 256), BF),...  103 us

profile of v7, /device:TPU:72, one launch (start us, length us, event | category | flops | bytes accessed | tf_op | source)
XLA Modules:
  0.0 104.2 jit_solution(1699745145170910346)
XLA Ops:
  0.0 102.6 %decode_block.1 = bf16[160,256]{1,0:T(8,128)(2,1)} custom-call(s32[4,40]{1,0:T(4,128)} %tok_ref.1, s32[1,40]{1,0:T(1,128)} %bitcast.9, bf16[16,81920]{1,0:T(8,128)(2,1)} %bitcast.5, bf16[256]{0:T(256)(128)(2,1)} %gain_ref.1, f32[1,128]{1,0:T(1,128)} %constant.2.clone.freq_ref, bf16[512,256]{1,0:T(8,128)(2,1)} %wq_ref.1, bf16[64,512]{1,0:T(8,128)(2,1)} %bitcast.8, ...), custom_call_target="tpu_custom_call" | custom-call | tf_op jit(solution)/shard_map/decode_block/pallas_call | solution.py:650
  102.6 1.5 %copy.11 = bf16[4,40,256]{2,1,0:T(8,128)(2,1)} copy(bf16[4,40,256]{2,1,0:T(8,128)(2,1)} %bitcast.7) | data formatting | bytes 163840
